TPU v7x, 128 devices: a whole 4x4x4 slice. The times are simulated.
128 devices in a mesh: space: 16 (over y, x_hi, core), member: 8 (over z, x_lo).
Axes of the slice: x: 4 (x_hi: 2, x_lo: 2; x = x_hi * 2 + x_lo), y: 4, z: 4, core: 2. Of those that a mesh axis runs over, the one named last changes fastest.
Arguments:
- temp_start: float32 [16, 10, 640, 640], P('member', None, 'space'), may hold values from -6 to 6
- cotangent: float32 [16, 10, 640, 640], P('member', None, 'space'), may hold values from -6 to 6
- forcing: float32 [16, 640, 640], P('member', 'space'), may hold values from -2 to 2
- soil_class: int32 [640, 640], P('space'), may hold values from 0 to 11
- conductivity: float32 [12, 10], replicated, may hold values from 0.03 to 0.18
- parent_field: float32 [10, 32, 32], P(None, 'space'), may hold values from -6 to 6
- tile_map: int32 [16], replicated, may hold values from 0 to 15, as said below
Outputs:
- temp_final: float32 [16, 10, 640, 640], P('member', None, 'space')
- adjoint_start: float32 [16, 10, 640, 640], P('member', None, 'space')
- parent_grad: float32 [10, 32, 32], P(None, 'space')
Inputs may be any that keep to these rules, and one draw needn't show every extreme that they name: `tile_map`: each parent tile holds exactly one nest tile.
All inputs are finite; a program needn't handle non-finite values.
Results may differ from a plain program's by a relative error of at most 0.00013.
Values sent between devices are 32-bit elements; how exact they have to be, the bound alone decides.
No kernel may reach another device: no remote copies, remote signals or barrier semaphores. Data moves between devices by JAX's collectives and lax.ppermute only.
A program may use at most 128 MiB of HBM per device.

v0:
```python
import jax
import jax.numpy as jnp
from jax import lax
from jax.sharding import PartitionSpec as P

R = 20
ITERS = 4


relax_rate = 0.1
vertical_rate = 0.05


def with_halo(value, sides, width):
    for axis, dim in sides:
        peers, length = (lax.axis_size(axis), value.shape[dim])
        up = [(i, (i + 1) % peers) for i in range(peers - 1)]
        down = [(j, i) for i, j in up]
        last = lax.slice_in_dim(value, length - width, length, axis=dim)
        initial = lax.slice_in_dim(value, 0, width, axis=dim)
        before = lax.ppermute(last, axis, up)
        after = lax.ppermute(initial, axis, down)
        value = jnp.concatenate([before, value, after], axis=dim)
    return value


def vertical_term(field):
    above_layer = jnp.concatenate([field[:, :1], field[:, :-1]], 1)
    below_layer = jnp.concatenate([field[:, 1:], field[:, -1:]], 1)
    return above_layer + below_layer - 2.0 * field


def planar_rows(extended):
    middle = extended[:, :, 1:-1]
    sides = jnp.pad(middle, ((0, 0), (0, 0), (0, 0), (1, 1)))
    total = extended[:, :, 2:] + extended[:, :, :-2]
    total = total + sides[..., 2:] + sides[..., :-2]
    return total - 4.0 * middle


def forward_rows(extended, kappa_rows, target_rows, forcing_rows):
    middle = extended[:, :, 1:-1]
    layer_top = (jnp.arange(middle.shape[1]) == 0)[None, :, None, None]
    updated = (
        middle
        + kappa_rows * planar_rows(extended)
        + vertical_rate * vertical_term(middle)
        + relax_rate * (target_rows - middle)
    )
    return updated + jnp.where(layer_top, forcing_rows[:, None], jnp.zeros((), jnp.float32))


def adjoint_rows(extended, kappa_ext):
    middle = extended[:, :, 1:-1]
    weighted = kappa_ext * extended
    return (
        middle + planar_rows(weighted) + vertical_rate * vertical_term(middle) - relax_rate * middle
    )


def body(temp_start, cotangent, forcing, soil_class, conductivity, parent_field, tile_map):
    layer_count = temp_start.shape[1]
    space_count = lax.axis_size("space")
    position = lax.axis_index("space")
    class_onehot = (
        soil_class[None, :, :] == jnp.arange(conductivity.shape[0], dtype=jnp.int32)[:, None, None]
    ).astype(jnp.float32)
    kappa = jnp.einsum("cl,cxy->lxy", conductivity, class_onehot, precision=lax.Precision.HIGHEST)
    rows_per = parent_field.shape[1]
    gathered = lax.all_gather(parent_field, "space", axis=1, tiled=True)
    owner_tile = lax.dynamic_slice_in_dim(tile_map, position, 1, 0)[0]
    parent_rows = lax.dynamic_slice_in_dim(gathered, owner_tile * rows_per, rows_per, 1)
    target = jnp.repeat(jnp.repeat(parent_rows, R, axis=1), R, axis=2)
    temp = temp_start
    adjoint = cotangent
    running = cotangent
    kappa_ext = with_halo(kappa, (("space", 1),), 1)
    for section in range(ITERS):
        extended = with_halo(temp, (("space", 2),), 1)
        temp = forward_rows(extended, kappa, target, forcing)
    for section in range(ITERS):
        extended = with_halo(adjoint, (("space", 2),), 1)
        adjoint = adjoint_rows(extended, kappa_ext)
        if section < ITERS - 1:
            running = running + adjoint
    summed = jnp.sum(running, 0)
    blocks = summed.reshape(layer_count, rows_per, R, summed.shape[2] // R, R).sum(axis=(2, 4)) * (
        relax_rate / (R * R)
    )
    empty_grad = jnp.zeros((layer_count, space_count * rows_per, blocks.shape[2]), jnp.float32)
    contribution = lax.dynamic_update_slice_in_dim(empty_grad, blocks, owner_tile * rows_per, 1)
    member_sum = lax.psum(contribution, "member")
    parent_grad = lax.psum_scatter(member_sum, "space", scatter_dimension=1, tiled=True)
    return (temp, adjoint, parent_grad)


def solution(mesh):
    return jax.shard_map(
        body,
        mesh=mesh,
        in_specs=(
            P("member", None, "space", None),
            P("member", None, "space", None),
            P("member", "space", None),
            P("space", None),
            P(),
            P(None, "space", None),
            P(),
        ),
        out_specs=(
            P("member", None, "space", None),
            P("member", None, "space", None),
            P(None, "space", None),
        ),
        check_vma=False,
    )
```

profile of v0, /device:TPU:0, one launch (start us, length us, event | category | flops | bytes accessed | tf_op | source)
XLA Modules:
  0.0 263.2 jit_solution(15289100015049988828)
XLA Ops:
  14.1 6.4 %collective-permute-start.10 = (f32[2,10,1,640]{3,2,1,0:T(1,128)}, f32[2,10,1,640]{3,2,1,0:T(1,128)S(1)}, u32[]{:S(2)}, u32[]{:S(2)}) collective-permute-start(f32[2,10,1,640]{3,2,1,0:T(1,128)} %get-tuple-element.33), channel_id=1, source_target_pairs={{0,8},{8,16},{16,24},{24,32},{32,40},{40,48},{48,56},{56,64},{64,7... | collective-permute-start | bytes 153608 | tf_op jit(solution)/shard_map/ppermute | solution.py:21
  24.9 2.1 fusion.86
  31.9 30.3 %all_gather.3 = f32[10,32,32]{2,0,1:T(8,128)S(1)} all-gather(f32[10,2,32]{2,0,1:T(8,128)S(1)} %copy.28), channel_id=1, replica_groups=mesh['space'=16,'member'=8] {'space'}, dimensions={1}, use_global_device_ids=true | all-gather | bytes 43520 | tf_op jit(solution)/shard_map/all_gather | solution.py:70
  62.2 2.8 %copy.27 = f32[10,40,640]{2,1,0:T(8,128)} copy(f32[10,40,640]{2,0,1:T(8,128)} %copy-done.13) | data formatting | bytes 2048000 | tf_op jit(solution)/shard_map/cl,cxy->lxy/dot_general | solution.py:68
  65.1 2.2 broadcast_in_dim.69
  67.3 4.5 %sub.90 = f32[10,40,640]{1,2,0:T(8,128)} reshape(f32[10,40,32,20]{1,3,2,0:T(8,128)} %broadcast_in_dim.69) | data formatting | bytes 2048000 | tf_op jit(solution)/shard_map/sub | solution.py:48
  71.8 3.2 %copy.31 = f32[10,40,640]{2,1,0:T(8,128)} copy(f32[10,40,640]{1,2,0:T(8,128)} %sub.90) | data formatting | bytes 2048000 | tf_op jit(solution)/shard_map/sub | solution.py:48
  75.0 2.2 collective-permute-start.1
  87.8 3.2 %select_add_fusion.3 = f32[2,10,40,640]{3,2,1,0:T(8,128)S(1)} fusion(f32[2,10,40,640]{3,2,1,0:T(8,128)S(1)} %copy-done.12, f32[2,10,1,640]{3,2,1,0:T(1,128)S(1)} %collective-permute-done.1, f32[2,10,1,640]{3,2,1,0:T(1,128)} %collective-permute-done, f32[2,9,40,640]{3,2,1,0:T(8,128)S(1)} %copy-done.15, f32[2,1,40,640]{3,2,1,0:T(8,128)S(1)} %copy-done.25, ...), kind=kLoop, calls=%fused_computation.3 | loop fusion | flops 10752000 | bytes 10547210 | tf_op jit(solution)/shard_map/add | solution.py:50
  95.9 3.7 %collective-permute-start.3 = (f32[2,10,1,640]{3,2,1,0:T(1,128)S(1)}, f32[2,10,1,640]{3,2,1,0:T(1,128)S(1)}, u32[]{:S(2)}, u32[]{:S(2)}) collective-permute-start(f32[2,10,1,640]{3,2,1,0:T(1,128)S(1)} %get-tuple-element.52), channel_id=1, source_target_pairs={{0,8},{8,16},{16,24},{24,32},{32,40},{40,48},{48,56},{56,64},{64,7... | collective-permute-start | bytes 153608 | tf_op jit(solution)/shard_map/ppermute | solution.py:21
  102.6 2.4 select_add_fusion.2
  105.2 5.1 %collective-permute-start.14 = (f32[2,10,1,640]{3,2,1,0:T(1,128)S(1)}, f32[2,10,1,640]{3,2,1,0:T(1,128)S(1)}, u32[]{:S(2)}, u32[]{:S(2)}) collective-permute-start(f32[2,10,1,640]{3,2,1,0:T(1,128)S(1)} %get-tuple-element.17), channel_id=1, source_target_pairs={{0,8},{8,16},{16,24},{24,32},{32,40},{40,48},{48,56},{56,64},{64,7... | collective-permute-start | bytes 153608 | tf_op jit(solution)/shard_map/ppermute | solution.py:21
  113.0 5.3 %collective-permute-start.5 = (f32[2,10,1,640]{3,2,1,0:T(1,128)S(1)}, f32[2,10,1,640]{3,2,1,0:T(1,128)S(1)}, u32[]{:S(2)}, u32[]{:S(2)}) collective-permute-start(f32[2,10,1,640]{3,2,1,0:T(1,128)S(1)} %get-tuple-element.46), channel_id=1, source_target_pairs={{0,8},{8,16},{16,24},{24,32},{32,40},{40,48},{48,56},{56,64},{64,7... | collective-permute-start | bytes 153608 | tf_op jit(solution)/shard_map/ppermute | solution.py:21
  118.9 3.3 %add_reduce_fusion = (f32[10,40,640]{2,1,0:T(8,128)}, f32[2,10,40,640]{3,2,1,0:T(8,128)S(1)}) fusion(f32[2,10,40,640]{3,2,1,0:T(8,128)S(1)} %fusion.39, f32[2,10,40,640]{3,2,1,0:T(8,128)S(1)} %copy-done.2, f32[2,10,40,640]{3,2,1,0:T(8,128)S(1)} %fusion.33, f32[2,1,40,640]{3,2,1,0:T(8,128)S(1)} %get-tuple-element.20, ...), kind=kLoop, calls=%fused_computation.116 | loop fusion | flops 9472000 | bytes 19456000 | tf_op jit(solution)/shard_map/reduce_sum | solution.py:86
  122.3 2.3 fusion.77
  126.1 2.4 select_add_fusion.1
  132.1 5.1 %collective-permute-start.16 = (f32[2,10,1,640]{3,2,1,0:T(1,128)}, f32[2,10,1,640]{3,2,1,0:T(1,128)S(1)}, u32[]{:S(2)}, u32[]{:S(2)}) collective-permute-start(f32[2,10,1,640]{3,2,1,0:T(1,128)} %get-tuple-element.15), channel_id=1, source_target_pairs={{0,8},{8,16},{16,24},{24,32},{32,40},{40,48},{48,56},{56,64},{64,7... | collective-permute-start | bytes 153608 | tf_op jit(solution)/shard_map/ppermute | solution.py:21
  138.5 9.4 %reshape.24 = f32[10,2,20,32,20]{4,3,2,1,0:T(8,128)} reshape(f32[10,40,640]{2,1,0:T(8,128)S(1)} %copy-done.22) | data formatting | bytes 2048000 | tf_op jit(solution)/shard_map/reshape | solution.py:87
  147.9 3.6 %reduce_sum.19 = f32[10,2,32]{2,1,0:T(2,128)S(1)} reduce(f32[10,2,20,32,20]{4,3,2,1,0:T(8,128)} %reshape.24, f32[]{:T(128)} %constant.12.clone.1), dimensions={2,4}, to_apply=%region_1.2 | reduce | flops 255360 | bytes 1026564 | tf_op jit(solution)/shard_map/reduce_sum | solution.py:87
  154.2 3.7 %collective-permute-start.7 = (f32[2,10,1,640]{3,2,1,0:T(1,128)}, f32[2,10,1,640]{3,2,1,0:T(1,128)S(1)}, u32[]{:S(2)}, u32[]{:S(2)}) collective-permute-start(f32[2,10,1,640]{3,2,1,0:T(1,128)} %get-tuple-element.40), channel_id=1, source_target_pairs={{0,8},{8,16},{16,24},{24,32},{32,40},{40,48},{48,56},{56,64},{64,7... | collective-permute-start | bytes 153608 | tf_op jit(solution)/shard_map/ppermute | solution.py:21
  161.6 3.3 %select_add_fusion = f32[2,10,40,640]{3,2,1,0:T(8,128)} fusion(f32[2,10,40,640]{3,2,1,0:T(8,128)S(1)} %copy-done.6, f32[2,10,1,640]{3,2,1,0:T(1,128)S(1)} %collective-permute-done.7, f32[2,10,1,640]{3,2,1,0:T(1,128)S(1)} %collective-permute-done.6, f32[2,9,40,640]{3,2,1,0:T(8,128)S(1)} %copy-done.21, f32[2,1,40,640]{3,2,1,0:T(8,128)S(1)} %copy-done.27, ...), kind=kLoop, calls=%fused_computation | loop fusion | flops 10752000 | bytes 10547210 | tf_op jit(solution)/shard_map/add | solution.py:50
  165.0 3.0 %fusion.51 = f32[2,10,40,640]{3,2,1,0:T(8,128)} fusion(f32[2,10,40,640]{3,2,1,0:T(8,128)S(1)} %copy-done.4, f32[2,10,40,640]{3,2,1,0:T(8,128)S(1)} %slice.397, f32[2,10,42,640]{3,2,1,0:T(8,128)S(1)} %maximum_multiply_fusion.3, f32[2,9,40,640]{3,2,1,0:T(8,128)S(1)} %copy-done.17, f32[2,1,40,640]{3,2,1,0:T(8,128)S(1)} %copy-done.29, ...), kind=kLoop, calls=%fused_computation.75 | loop fusion | flops 7680000 | bytes 14336000 | tf_op jit(solution)/shard_map/sub | solution.py:57
  168.0 53.9 %reduce-scatter.2.cloned.1.call-done = f32[10,2,32]{2,0,1:T(8,128)} async-done(((f32[10,32,32]{2,0,1:T(8,128)}), f32[10,2,32]{2,0,1:T(8,128)}) %reduce-scatter.2.cloned.1.call-update) | async-done | bytes 2576 | tf_op jit(solution)/shard_map/reduce_scatter | solution.py:93
  221.8 33.9 %psum.8 = f32[10,2,32]{2,0,1:T(8,128)S(1)} all-reduce(f32[10,2,32]{2,0,1:T(8,128)} %reduce-scatter.2.cloned.1.call-done), channel_id=1, replica_groups=mesh['space'=16,'member'=8] {'member'}, use_global_device_ids=true, to_apply=%region_2.3 | all-reduce | flops 640 | bytes 5120 | tf_op jit(solution)/shard_map/psum | solution.py:92
  (149 shorter events, 50.4 us)
Async XLA Ops:
  7.2 17.7 %copy-start.2 = (f32[2,10,40,640]{3,2,1,0:T(8,128)S(1)}, f32[2,10,40,640]{3,2,1,0:T(8,128)}, u32[]{:S(2)}) copy-start(f32[2,10,40,640]{3,2,1,0:T(8,128)} %param.8) | copy-start | bytes 6144004
  7.2 214.7 %reduce-scatter.2.cloned.1.call-start = ((), (), s32[]{:S(2)}) async-start(), calls=%async_computation.1 | async-start | bytes 278528 | tf_op jit(solution)/shard_map/reduce_scatter | solution.py:93
  9.6 14.0 %copy-start.13 = (f32[10,40,640]{2,0,1:T(8,128)}, f32[10,40,640]{2,0,1:T(8,128)S(1)}, u32[]{:S(2)}) copy-start(f32[10,40,640]{2,0,1:T(8,128)S(1)} %fusion.73) | copy-start | bytes 3072004
  9.7 65.3 %collective-permute-start.8 = (f32[10,1,640]{2,0,1:T(8,128)S(1)}, f32[10,1,640]{2,0,1:T(8,128)S(1)}, u32[]{:S(2)}, u32[]{:S(2)}) collective-permute-start(f32[10,1,640]{2,0,1:T(8,128)S(1)} %get-tuple-element.59), channel_id=1, source_target_pairs={{0,8},{8,16},{16,24},{24,32},{32,40},{40,48},{48,56},{56,64},{64,7... | collective-permute-start | bytes 76808 | tf_op jit(solution)/shard_map/ppermute | solution.py:21
  11.0 66.3 %collective-permute-start.9 = (f32[10,1,640]{2,0,1:T(8,128)S(1)}, f32[10,1,640]{2,0,1:T(8,128)S(1)}, u32[]{:S(2)}, u32[]{:S(2)}) collective-permute-start(f32[10,1,640]{2,0,1:T(8,128)S(1)} %get-tuple-element.60), channel_id=1, source_target_pairs={{8,0},{16,8},{24,16},{32,24},{40,32},{48,40},{56,48},{64,56},{72,6... | collective-permute-start | bytes 76808 | tf_op jit(solution)/shard_map/ppermute | solution.py:22
  14.1 65.1 %collective-permute-start.10 = (f32[2,10,1,640]{3,2,1,0:T(1,128)}, f32[2,10,1,640]{3,2,1,0:T(1,128)S(1)}, u32[]{:S(2)}, u32[]{:S(2)}) collective-permute-start(f32[2,10,1,640]{3,2,1,0:T(1,128)} %get-tuple-element.33), channel_id=1, source_target_pairs={{0,8},{8,16},{16,24},{24,32},{32,40},{40,48},{48,56},{56,64},{64,7... | collective-permute-start | bytes 153608 | tf_op jit(solution)/shard_map/ppermute | solution.py:21
  20.5 58.7 %collective-permute-start.11 = (f32[2,10,1,640]{3,2,1,0:T(1,128)}, f32[2,10,1,640]{3,2,1,0:T(1,128)}, u32[]{:S(2)}, u32[]{:S(2)}) collective-permute-start(f32[2,10,1,640]{3,2,1,0:T(1,128)} %get-tuple-element.34), channel_id=1, source_target_pairs={{8,0},{16,8},{24,16},{32,24},{40,32},{48,40},{56,48},{64,56},{72,6... | collective-permute-start | bytes 153608 | tf_op jit(solution)/shard_map/ppermute | solution.py:22
  23.6 61.3 %collective-permute-start = (f32[2,10,1,640]{3,2,1,0:T(1,128)}, f32[2,10,1,640]{3,2,1,0:T(1,128)}, u32[]{:S(2)}, u32[]{:S(2)}) collective-permute-start(f32[2,10,1,640]{3,2,1,0:T(1,128)} %get-tuple-element.57), channel_id=1, source_target_pairs={{8,0},{16,8},{24,16},{32,24},{40,32},{48,40},{56,48},{64,56},{72,6... | collective-permute-start | bytes 153608 | tf_op jit(solution)/shard_map/ppermute | solution.py:22
  62.2 63.9 %copy-start.32 = (pred[10]{0:T(512)(128)(4,1)}, pred[10]{0:T(512)(128)(4,1)S(1)}, u32[]{:S(2)}) copy-start(pred[10]{0:T(512)(128)(4,1)S(1)} %iota_compare_fusion.4) | copy-start | bytes 34
  75.0 9.9 %collective-permute-start.1 = (f32[2,10,1,640]{3,2,1,0:T(1,128)}, f32[2,10,1,640]{3,2,1,0:T(1,128)S(1)}, u32[]{:S(2)}, u32[]{:S(2)}) collective-permute-start(f32[2,10,1,640]{3,2,1,0:T(1,128)} %get-tuple-element.58), channel_id=1, source_target_pairs={{0,8},{8,16},{16,24},{24,32},{32,40},{40,48},{48,56},{56,64},{64,7... | collective-permute-start | bytes 153608 | tf_op jit(solution)/shard_map/ppermute | solution.py:21
  91.3 8.3 %collective-permute-start.12 = (f32[2,10,1,640]{3,2,1,0:T(1,128)S(1)}, f32[2,10,1,640]{3,2,1,0:T(1,128)S(1)}, u32[]{:S(2)}, u32[]{:S(2)}) collective-permute-start(f32[2,10,1,640]{3,2,1,0:T(1,128)S(1)} %get-tuple-element.27), channel_id=1, source_target_pairs={{0,8},{8,16},{16,24},{24,32},{32,40},{40,48},{48,56},{56,64},{64,7... | collective-permute-start | bytes 153608 | tf_op jit(solution)/shard_map/ppermute | solution.py:21
  93.2 6.4 %collective-permute-start.13 = (f32[2,10,1,640]{3,2,1,0:T(1,128)S(1)}, f32[2,10,1,640]{3,2,1,0:T(1,128)S(1)}, u32[]{:S(2)}, u32[]{:S(2)}) collective-permute-start(f32[2,10,1,640]{3,2,1,0:T(1,128)S(1)} %get-tuple-element.28), channel_id=1, source_target_pairs={{8,0},{16,8},{24,16},{32,24},{40,32},{48,40},{56,48},{64,56},{72,6... | collective-permute-start | bytes 153608 | tf_op jit(solution)/shard_map/ppermute | solution.py:22
  94.6 8.0 %collective-permute-start.2 = (f32[2,10,1,640]{3,2,1,0:T(1,128)S(1)}, f32[2,10,1,640]{3,2,1,0:T(1,128)S(1)}, u32[]{:S(2)}, u32[]{:S(2)}) collective-permute-start(f32[2,10,1,640]{3,2,1,0:T(1,128)S(1)} %get-tuple-element.51), channel_id=1, source_target_pairs={{8,0},{16,8},{24,16},{32,24},{40,32},{48,40},{56,48},{64,56},{72,6... | collective-permute-start | bytes 153608 | tf_op jit(solution)/shard_map/ppermute | solution.py:22
  95.9 6.7 %collective-permute-start.3 = (f32[2,10,1,640]{3,2,1,0:T(1,128)S(1)}, f32[2,10,1,640]{3,2,1,0:T(1,128)S(1)}, u32[]{:S(2)}, u32[]{:S(2)}) collective-permute-start(f32[2,10,1,640]{3,2,1,0:T(1,128)S(1)} %get-tuple-element.52), channel_id=1, source_target_pairs={{0,8},{8,16},{16,24},{24,32},{32,40},{40,48},{48,56},{56,64},{64,7... | collective-permute-start | bytes 153608 | tf_op jit(solution)/shard_map/ppermute | solution.py:21
  105.2 13.2 %collective-permute-start.14 = (f32[2,10,1,640]{3,2,1,0:T(1,128)S(1)}, f32[2,10,1,640]{3,2,1,0:T(1,128)S(1)}, u32[]{:S(2)}, u32[]{:S(2)}) collective-permute-start(f32[2,10,1,640]{3,2,1,0:T(1,128)S(1)} %get-tuple-element.17), channel_id=1, source_target_pairs={{0,8},{8,16},{16,24},{24,32},{32,40},{40,48},{48,56},{56,64},{64,7... | collective-permute-start | bytes 153608 | tf_op jit(solution)/shard_map/ppermute | solution.py:21
  110.4 8.0 %collective-permute-start.15 = (f32[2,10,1,640]{3,2,1,0:T(1,128)S(1)}, f32[2,10,1,640]{3,2,1,0:T(1,128)S(1)}, u32[]{:S(2)}, u32[]{:S(2)}) collective-permute-start(f32[2,10,1,640]{3,2,1,0:T(1,128)S(1)} %get-tuple-element.18), channel_id=1, source_target_pairs={{8,0},{16,8},{24,16},{32,24},{40,32},{48,40},{56,48},{64,56},{72,6... | collective-permute-start | bytes 153608 | tf_op jit(solution)/shard_map/ppermute | solution.py:22
  111.8 14.3 %collective-permute-start.4 = (f32[2,10,1,640]{3,2,1,0:T(1,128)S(1)}, f32[2,10,1,640]{3,2,1,0:T(1,128)S(1)}, u32[]{:S(2)}, u32[]{:S(2)}) collective-permute-start(f32[2,10,1,640]{3,2,1,0:T(1,128)S(1)} %get-tuple-element.45), channel_id=1, source_target_pairs={{8,0},{16,8},{24,16},{32,24},{40,32},{48,40},{56,48},{64,56},{72,6... | collective-permute-start | bytes 153608 | tf_op jit(solution)/shard_map/ppermute | solution.py:22
  113.0 13.0 %collective-permute-start.5 = (f32[2,10,1,640]{3,2,1,0:T(1,128)S(1)}, f32[2,10,1,640]{3,2,1,0:T(1,128)S(1)}, u32[]{:S(2)}, u32[]{:S(2)}) collective-permute-start(f32[2,10,1,640]{3,2,1,0:T(1,128)S(1)} %get-tuple-element.46), channel_id=1, source_target_pairs={{0,8},{8,16},{16,24},{24,32},{32,40},{40,48},{48,56},{56,64},{64,7... | collective-permute-start | bytes 153608 | tf_op jit(solution)/shard_map/ppermute | solution.py:21
  132.1 25.9 %collective-permute-start.16 = (f32[2,10,1,640]{3,2,1,0:T(1,128)}, f32[2,10,1,640]{3,2,1,0:T(1,128)S(1)}, u32[]{:S(2)}, u32[]{:S(2)}) collective-permute-start(f32[2,10,1,640]{3,2,1,0:T(1,128)} %get-tuple-element.15), channel_id=1, source_target_pairs={{0,8},{8,16},{16,24},{24,32},{32,40},{40,48},{48,56},{56,64},{64,7... | collective-permute-start | bytes 153608 | tf_op jit(solution)/shard_map/ppermute | solution.py:21
  137.2 20.7 %collective-permute-start.17 = (f32[2,10,1,640]{3,2,1,0:T(1,128)}, f32[2,10,1,640]{3,2,1,0:T(1,128)}, u32[]{:S(2)}, u32[]{:S(2)}) collective-permute-start(f32[2,10,1,640]{3,2,1,0:T(1,128)} %get-tuple-element.16), channel_id=1, source_target_pairs={{8,0},{16,8},{24,16},{32,24},{40,32},{48,40},{56,48},{64,56},{72,6... | collective-permute-start | bytes 153608 | tf_op jit(solution)/shard_map/ppermute | solution.py:22
  147.9 10.0 %copy-start.4 = (f32[2,10,40,640]{3,2,1,0:T(8,128)S(1)}, f32[2,10,40,640]{3,2,1,0:T(8,128)}, u32[]{:S(2)}) copy-start(f32[2,10,40,640]{3,2,1,0:T(8,128)} %copy-done.3) | copy-start | bytes 6144004
  152.9 6.6 %collective-permute-start.6 = (f32[2,10,1,640]{3,2,1,0:T(1,128)}, f32[2,10,1,640]{3,2,1,0:T(1,128)S(1)}, u32[]{:S(2)}, u32[]{:S(2)}) collective-permute-start(f32[2,10,1,640]{3,2,1,0:T(1,128)} %get-tuple-element.39), channel_id=1, source_target_pairs={{8,0},{16,8},{24,16},{32,24},{40,32},{48,40},{56,48},{64,56},{72,6... | collective-permute-start | bytes 153608 | tf_op jit(solution)/shard_map/ppermute | solution.py:22
  154.2 5.3 %collective-permute-start.7 = (f32[2,10,1,640]{3,2,1,0:T(1,128)}, f32[2,10,1,640]{3,2,1,0:T(1,128)S(1)}, u32[]{:S(2)}, u32[]{:S(2)}) collective-permute-start(f32[2,10,1,640]{3,2,1,0:T(1,128)} %get-tuple-element.40), channel_id=1, source_target_pairs={{0,8},{8,16},{16,24},{24,32},{32,40},{40,48},{48,56},{56,64},{64,7... | collective-permute-start | bytes 153608 | tf_op jit(solution)/shard_map/ppermute | solution.py:21
  165.0 91.4 %copy-start.1 = (f32[12,10]{1,0:T(8,128)S(1)}, f32[12,10]{1,0:T(8,128)}, u32[]{:S(2)}) copy-start(f32[12,10]{1,0:T(8,128)} %param.11) | copy-start | bytes 1444
  (30 other events, 82.4 us)
Sparse Core Ops, SparseCore 0:
  153.0 68.8 reduce-scatter.1
where the time goes:
time: 264 us; the launch traced here: 263 us
  blocking collectives  64.2 us (24%)
  waiting for transfers between devices  53.9 us (20%)
  local copies, waits for them, and re-layouts  51.3 us (19%)
  starting transfers between devices  46.5 us (18%)
  other arithmetic  30 us (11%)
  between operations  15.5 us (6%)
    reduce_scatter x1, waiting for transfers between devices, body(): lax.psum_scatter(member_sum, 'space', scatter_dimension=1, tiled=True)  53.9 us
    ppermute x9, starting transfers between devices, with_halo(): before = lax.ppermute(last, axis, up)  34.8 us
    psum x1, blocking collectives, body(): member_sum = lax.psum(contribution, 'member')  33.9 us
    all_gather x1, blocking collectives, body(): gathered = lax.all_gather(parent_field, 'space', axis=1, tiled=True)  30.3 us
    slice x14, local copies, waits for them, and re-layouts, vertical_term(): below_layer = jnp.concatenate([field[:, 1:], field[:, -1:]], 1)  12.4 us
    ppermute x9, starting transfers between devices, with_halo(): after = lax.ppermute(initial, axis, down)  11.6 us
    add x4, other arithmetic, forward_rows(): updated + jnp.where(layer_top, forcing_rows[:, None], jnp.zeros((), jnp.f...  11.3 us
    reshape x1, local copies, waits for them, and re-layouts, body(): summed.reshape(layer_count, rows_per, R, summed.shape[2] // R, R)  9.39 us
  transfers between devices with their start and end apart: 19, of which 1 were waited for; matrix products, arithmetic and copies ran while one was open for 23% of the time, Pallas kernels for 0%

commit v1 on v0

v1 whole, which is shorter than its diff:
```python
import functools

import jax
import jax.numpy as jnp
from jax import lax
from jax.experimental import pallas as pl
from jax.experimental.pallas import tpu as pltpu
from jax.sharding import PartitionSpec as P

R = 20
ITERS = 4
HALO = ITERS
LANES = 128
RELAX = 0.1
VERT = 0.05
KEEP = 1.0 - RELAX - 2.0 * VERT
f32 = jnp.float32
HIGHEST = lax.Precision.HIGHEST

VM = pl.BlockSpec(memory_space=pltpu.VMEM)
SM = pl.BlockSpec(memory_space=pltpu.SMEM)
HB = pl.BlockSpec(memory_space=pl.ANY)
PARAMS = pltpu.CompilerParams(vmem_limit_bytes=56 * 1024 * 1024)


def cols_of(c):
    return slice(c * LANES, (c + 1) * LANES)


def spread(group, rows, width):
    y = lax.broadcasted_iota(jnp.int32, (width, LANES), 0)
    lane = lax.broadcasted_iota(jnp.int32, (width, LANES), 1)
    return (y // rows + 32 * group == lane).astype(f32)


def pack_kernel(cot, temp, forcing, soil, parent, a_cot, b_cot, a_temp, b_temp, tiles, edge_c, edge_t, edge_f, edge_s, flat, sems):
    rows = cot.shape[2]
    odd = lax.axis_index("space") % 2
    copies = []
    for side, start in ((0, 0), (1, rows - 8)):
        cut = pl.ds(start, 8)
        copies.append(pltpu.make_async_copy(cot.at[:, :, cut, :], edge_c.at[side], sems.at[side, 0]))
        copies.append(pltpu.make_async_copy(soil.at[cut, :], edge_s.at[side], sems.at[side, 1]))
        copies.append(pltpu.make_async_copy(temp.at[:, :, cut, :], edge_t.at[side], sems.at[side, 2]))
        copies.append(pltpu.make_async_copy(forcing.at[:, cut, :], edge_f.at[side], sems.at[side, 3]))
    for copy in copies:
        copy.start()
    members, layers = cot.shape[:2]
    groups = -(-2 * layers // 8)
    flat[...] = jnp.zeros_like(flat)
    for l in range(layers):
        flat[2 * l:2 * l + 2, :] = parent[l]
    packed = jnp.zeros((8, LANES), f32)
    for g in range(groups):
        packed = packed + jnp.dot(flat[8 * g:8 * g + 8, :], spread(g, 1, flat.shape[1]), precision=HIGHEST)
    for i in range(tiles.shape[0]):
        tiles[i] = packed
    for copy in copies:
        copy.wait()
    for parity in (0, 1):
        @pl.when(odd == parity)
        def _():
            low, high = (slice(0, 4), slice(4, 8))
            for side, cut in ((0, low), (1, high)):
                to_a = (side == 1) == (parity == 0)
                oc, ot = (a_cot, a_temp) if to_a else (b_cot, b_temp)
                for m in range(members):
                    for l in range(layers):
                        oc[m * layers + l] = edge_c[side, m, l, cut, :]
                        ot[m * layers + l] = edge_t[side, m, l, cut, :]
                    ot[members * layers + m] = edge_f[side, m, cut, :]
                oc[members * layers] = edge_s[side, cut, :].astype(f32) + 1.0


def side_rows(odd, a_ref, b_ref, p):
    a, b = a_ref[p], b_ref[p]
    return jnp.where(odd == 1, a, b), jnp.where(odd == 1, b, a)


def fill_kappa(soil, a_cot, b_cot, cond, odd, layers, S, K, C):
    rows, cols = soil.shape
    top, bottom = side_rows(odd, a_cot, b_cot, a_cot.shape[0] - 1)
    lane = lax.broadcasted_iota(jnp.int32, (8, LANES), 1)
    for c in range(cols // LANES):
        S[c, 0:HALO, :] = top[:, cols_of(c)].astype(jnp.int32) - 1
        S[c, rows + HALO:, :] = bottom[:, cols_of(c)].astype(jnp.int32) - 1
        S[c, HALO:rows + HALO, :] = soil[:, cols_of(c)]
    classes = cond.shape[0]
    for l in range(layers):
        table = jnp.zeros((8, LANES), f32)
        for k in range(classes):
            table = jnp.where(lane == k, cond[k, l], table)
        for c in range(cols // LANES):
            for i in range((rows + 2 * HALO) // 8):
                cut = slice(8 * i, 8 * i + 8)
                idx = S[c, cut, :]
                idx = jnp.where(idx < 0, LANES - 1, idx)
                kappa = jnp.take_along_axis(table, idx, axis=1)
                K[l, c, cut, :] = kappa
                C[l, c, cut, :] = KEEP - 4.0 * kappa


def fill_field(field, a_ref, b_ref, odd, X):
    members, layers, rows, cols = field.shape

    def plane(p, carry):
        top, bottom = side_rows(odd, a_ref, b_ref, p)
        for c in range(cols // LANES):
            X[0, p, c, 0:HALO, :] = top[:, cols_of(c)]
            X[0, p, c, rows + HALO:, :] = bottom[:, cols_of(c)]
            X[0, p, c, HALO:rows + HALO, :] = field[p // layers, p % layers, :, cols_of(c)]
        return carry

    lax.fori_loop(0, members * layers, plane, 0)


def sideways(center):
    lane = lax.broadcasted_iota(jnp.int32, (8, LANES), 1)
    count = len(center)
    right = [pltpu.roll(v, 1, 1) for v in center]
    left = [pltpu.roll(v, LANES - 1, 1) for v in center]
    out = []
    for c in range(count):
        before = right[c - 1] if c > 0 else jnp.zeros((8, LANES), f32)
        after = left[c + 1] if c < count - 1 else jnp.zeros((8, LANES), f32)
        out.append(jnp.where(lane == 0, before, right[c]) + jnp.where(lane == LANES - 1, after, left[c]))
    return out


def chunk_start(i, rows):
    return jnp.minimum(1 + 8 * i, rows + 2 * HALO - 9)


def adjoint_kernel(cot, a_cot, b_cot, soil, cond, tile_map, adj, blocks, X, W, K, C, S, RS, BS):
    members, layers, rows, cols = cot.shape
    position = lax.axis_index("space")
    odd = position % 2
    nb = cols // LANES
    chunks = RS.shape[0]
    fill_kappa(soil, a_cot, b_cot, cond, odd, layers, S, K, C)
    fill_field(cot, a_cot, b_cot, odd, X)

    def weigh(p, carry):
        for c in range(nb):
            W[0, p, c] = X[0, p, c] * K[p % layers, c]
        return carry

    lax.fori_loop(0, members * layers, weigh, 0)

    for k in range(ITERS):
        src, dst = k % 2, 1 - k % 2
        last = k == ITERS - 1

        def chunk(i, carry):
            r = HALO + 8 * i if last else chunk_start(i, rows)
            mid, up, down = pl.ds(r, 8), pl.ds(r - 1, 8), pl.ds(r + 1, 8)
            above = [[X[src, m * layers, c, mid, :] for c in range(nb)] for m in range(members)]
            here = above
            for l in range(layers):
                total = [None] * nb
                after = []
                for m in range(members):
                    p = m * layers + l
                    below = [X[src, p + 1, c, mid, :] for c in range(nb)] if l < layers - 1 else here[m]
                    after.append(below)
                    side = sideways([W[src, p, c, mid, :] for c in range(nb)])
                    for c in range(nb):
                        planar = side[c] + (W[src, p, c, up, :] + W[src, p, c, down, :])
                        new = C[l, c, mid, :] * here[m][c] + planar + VERT * (above[m][c] + below[c])
                        if l == 0 or l == layers - 1:
                            pass
                        if last:
                            adj[m, l, pl.ds(pl.multiple_of(8 * i, 8), 8), cols_of(c)] = new
                        else:
                            X[dst, p, c, mid, :] = new
                            W[dst, p, c, mid, :] = K[l, c, mid, :] * new
                            part = new + here[m][c] if k == 0 else new
                            total[c] = part if total[c] is None else total[c] + part
                if not last:
                    for c in range(nb):
                        RS[i, l, c] = total[c] if k == 0 else RS[i, l, c] + total[c]
                above, here = here, after
            return carry

        lax.fori_loop(0, rows // 8 if last else chunks, chunk, 0)
        if k == ITERS - 2:
            row = lax.broadcasted_iota(jnp.int32, (8, LANES), 0)
            BS[...] = jnp.zeros_like(BS)
            for l in range(layers):
                for c in range(nb):
                    sums = [jnp.zeros((8, LANES), f32)] * 2
                    done = HALO
                    for i in range(chunks):
                        start = min(1 + 8 * i, rows + 2 * HALO - 9)
                        value = RS[i, l, c]
                        for b in range(2):
                            lo = max(done, HALO + R * b) - start
                            hi = min(start + 8, HALO + R * (b + 1)) - start
                            if hi <= max(lo, 0):
                                continue
                            part = value if lo <= 0 and hi >= 8 else jnp.where((row >= lo) & (row < hi), value, 0.0)
                            sums[b] = sums[b] + part
                        done = start + 8
                    for b in range(2):
                        BS[2 * l + b:2 * l + b + 1, cols_of(c)] = jnp.sum(sums[b], axis=0, keepdims=True)
            packed = jnp.zeros((8, LANES), f32)
            for g in range(BS.shape[0] // 8):
                packed = packed + jnp.dot(BS[8 * g:8 * g + 8, :], spread(g, R, cols), precision=HIGHEST)
            packed = packed * (RELAX / (R * R))
            blocks[...] = jnp.zeros_like(blocks)
            spaces = tile_map.shape[0]
            owner = tile_map[position]
            for m in range(blocks.shape[0] // spaces):
                blocks[m * spaces + owner] = packed


def forward_kernel(temp, forcing, a_temp, b_temp, a_cot, b_cot, soil, cond, tiles, tile_map, out, X, K, C, S, T, F, TE):
    members, layers, rows, cols = temp.shape
    spaces = tile_map.shape[0]
    position = lax.axis_index("space")
    odd = position % 2
    nb = cols // LANES
    ext = rows + 2 * HALO
    fill_kappa(soil, a_cot, b_cot, cond, odd, layers, S, K, C)
    fill_field(temp, a_temp, b_temp, odd, X)
    around = []
    for shift in (-1, 0, 1):
        where = jnp.minimum(jnp.maximum(position + shift, 0), spaces - 1)
        inside = jnp.logical_and(position + shift >= 0, position + shift < spaces)
        around.append(jnp.where(inside, tiles[tile_map[where]], 0.0))
    stack = jnp.concatenate(around, axis=0) * RELAX
    for g in range(TE.shape[0]):
        lane = lax.broadcasted_iota(jnp.int32, (LANES, cols), 0)
        y = lax.broadcasted_iota(jnp.int32, (LANES, cols), 1)
        TE[g] = jnp.dot(stack, (y // R + 32 * g == lane).astype(f32), precision=HIGHEST)

    def levels(l, t, b):
        n = 2 * l + b
        return TE[n // 8, 8 * t + n % 8:8 * t + n % 8 + 1, :]

    for l in range(layers):
        bands = [(0, HALO, levels(l, 0, 1)), (HALO, HALO + R, levels(l, 1, 0)), (HALO + R, HALO + 2 * R, levels(l, 1, 1)), (HALO + 2 * R, ext, levels(l, 2, 0))]
        for c in range(nb):
            for lo, hi, value in bands:
                T[l, c, lo:hi, :] = jnp.broadcast_to(value[:, cols_of(c)], (hi - lo, LANES))
    for m in range(members):
        top, bottom = side_rows(odd, a_temp, b_temp, members * layers + m)
        for c in range(nb):
            F[m, c, 0:HALO, :] = T[0, c, 0:HALO, :] + top[:, cols_of(c)]
            F[m, c, rows + HALO:, :] = T[0, c, rows + HALO:, :] + bottom[:, cols_of(c)]
            F[m, c, HALO:rows + HALO, :] = T[0, c, HALO:rows + HALO, :] + forcing[m, :, cols_of(c)]

    for k in range(ITERS):
        src, dst = k % 2, 1 - k % 2
        last = k == ITERS - 1

        def chunk(i, carry):
            r = HALO + 8 * i if last else chunk_start(i, rows)
            mid, up, down = pl.ds(r, 8), pl.ds(r - 1, 8), pl.ds(r + 1, 8)
            above = [[X[src, m * layers, c, mid, :] for c in range(nb)] for m in range(members)]
            here = above
            for l in range(layers):
                after = []
                for m in range(members):
                    p = m * layers + l
                    below = [X[src, p + 1, c, mid, :] for c in range(nb)] if l < layers - 1 else here[m]
                    after.append(below)
                    side = sideways(here[m])
                    for c in range(nb):
                        around = side[c] + (X[src, p, c, up, :] + X[src, p, c, down, :])
                        source = F[m, c, mid, :] if l == 0 else T[l, c, mid, :]
                        new = C[l, c, mid, :] * here[m][c] + K[l, c, mid, :] * around + (VERT * (above[m][c] + below[c]) + source)
                        if last:
                            out[m, l, pl.ds(pl.multiple_of(8 * i, 8), 8), cols_of(c)] = new
                        else:
                            X[dst, p, c, mid, :] = new
                above, here = here, after
            return carry

        lax.fori_loop(0, rows // 8 if last else -(-(ext - 2) // 8), chunk, 0)


def sum_kernel(received, out, total):
    value = received[0]
    for i in range(1, received.shape[0]):
        value = value + received[i]
    total[...] = value
    layers, per, width = out.shape
    for l in range(layers):
        for b in range(per):
            n = per * l + b
            out[l, b:b + 1, :] = total[n % 8:n % 8 + 1, 32 * (n // 8):32 * (n // 8) + width]


def body(temp_start, cotangent, forcing, soil_class, conductivity, parent_field, tile_map):
    members, layers, rows, cols = temp_start.shape
    nb = cols // LANES
    spaces = lax.axis_size("space")
    groups = lax.axis_size("member")
    planes = members * layers
    ext = rows + 2 * HALO
    chunks = -(-(ext - 2) // 8)
    pieces = -(-2 * layers // 8)
    shape = lambda *dims: jax.ShapeDtypeStruct(dims, f32)
    a_cot, b_cot, a_temp, b_temp, tiles = pl.pallas_call(
        pack_kernel,
        out_shape=(shape(planes + 1, HALO, cols), shape(planes + 1, HALO, cols), shape(planes + members, HALO, cols), shape(planes + members, HALO, cols), shape(spaces, 8, LANES)),
        in_specs=[HB, HB, HB, HB, VM],
        out_specs=[VM] * 5,
        scratch_shapes=[
            pltpu.VMEM((2, members, layers, 8, cols), f32),
            pltpu.VMEM((2, members, layers, 8, cols), f32),
            pltpu.VMEM((2, members, 8, cols), f32),
            pltpu.VMEM((2, 8, cols), jnp.int32),
            pltpu.VMEM((8 * pieces, parent_field.shape[2]), f32),
            pltpu.SemaphoreType.DMA((2, 4)),
        ],
        compiler_params=PARAMS,
        name="pack",
    )(cotangent, temp_start, forcing, soil_class, parent_field)
    pair = [(i, i ^ 1) for i in range(spaces)]
    across = [(i, i + 1) for i in range(1, spaces - 1, 2)] + [(i + 1, i) for i in range(1, spaces - 1, 2)]
    a_cot = lax.ppermute(a_cot, "space", pair)
    b_cot = lax.ppermute(b_cot, "space", across)
    a_temp = lax.ppermute(a_temp, "space", pair)
    b_temp = lax.ppermute(b_temp, "space", across)
    tiles = lax.all_to_all(tiles, "space", 0, 0, tiled=True)
    flops = 15 * planes * ext * cols * ITERS
    cost = pl.CostEstimate(flops=flops, bytes_accessed=4 * 2 * planes * rows * cols, transcendentals=0)
    adjoint, blocks = pl.pallas_call(
        adjoint_kernel,
        out_shape=(jax.ShapeDtypeStruct(cotangent.shape, f32), shape(groups * spaces, 8, LANES)),
        in_specs=[VM, VM, VM, VM, SM, SM],
        out_specs=[VM, VM],
        scratch_shapes=[
            pltpu.VMEM((2, planes, nb, ext, LANES), f32),
            pltpu.VMEM((2, planes, nb, ext, LANES), f32),
            pltpu.VMEM((layers, nb, ext, LANES), f32),
            pltpu.VMEM((layers, nb, ext, LANES), f32),
            pltpu.VMEM((nb, ext, LANES), jnp.int32),
            pltpu.VMEM((chunks, layers, nb, 8, LANES), f32),
            pltpu.VMEM((8 * pieces, cols), f32),
        ],
        compiler_params=PARAMS,
        cost_estimate=cost,
        name="adjoint",
    )(cotangent, a_cot, b_cot, soil_class, conductivity, tile_map)
    received = lax.all_to_all(blocks, ("member", "space"), 0, 0, tiled=True)
    temp = pl.pallas_call(
        forward_kernel,
        out_shape=jax.ShapeDtypeStruct(temp_start.shape, f32),
        in_specs=[VM, VM, VM, VM, VM, VM, VM, SM, VM, SM],
        out_specs=VM,
        scratch_shapes=[
            pltpu.VMEM((2, planes, nb, ext, LANES), f32),
            pltpu.VMEM((layers, nb, ext, LANES), f32),
            pltpu.VMEM((layers, nb, ext, LANES), f32),
            pltpu.VMEM((nb, ext, LANES), jnp.int32),
            pltpu.VMEM((layers, nb, ext, LANES), f32),
            pltpu.VMEM((members, nb, ext, LANES), f32),
            pltpu.VMEM((pieces, 24, cols), f32),
        ],
        compiler_params=PARAMS,
        cost_estimate=cost,
        name="forward",
    )(temp_start, forcing, a_temp, b_temp, a_cot, b_cot, soil_class, conductivity, tiles, tile_map)
    parent_grad = pl.pallas_call(
        sum_kernel,
        out_shape=shape(*parent_field.shape),
        in_specs=[VM],
        out_specs=VM,
        scratch_shapes=[pltpu.VMEM((8, LANES), f32)],
        compiler_params=PARAMS,
        name="collect",
    )(received)
    return temp, adjoint, parent_grad


def solution(mesh):
    return jax.shard_map(
        body,
        mesh=mesh,
        in_specs=(
            P("member", None, "space", None),
            P("member", None, "space", None),
            P("member", "space", None),
            P("space", None),
            P(),
            P(None, "space", None),
            P(),
        ),
        out_specs=(
            P("member", None, "space", None),
            P("member", None, "space", None),
            P(None, "space", None),
        ),
        check_vma=False,
    )
```

time: 264 us -> 70.3 us (0.27)
  the two profiles are of different devices: /device:TPU:0 before, /device:TPU:1 now
where the time goes in v1:
time: 70.3 us; the launch traced here: 69.9 us
  Pallas kernels  29.7 us (42%)
  starting transfers between devices  27.9 us (40%)
  waiting for transfers between devices  9.26 us (13%)
  local copies, waits for them, and re-layouts  2.25 us (3%)
  between operations  0.73 us (1%)
    pallas_call x1, Pallas kernels, body(): pl.pallas_call(forward_kernel, out_shape=jax.ShapeDtypeStruct(temp_start....  12.4 us
    pallas_call x1, Pallas kernels, body(): pl.pallas_call(adjoint_kernel, out_shape=(jax.ShapeDtypeStruct(cotangent....  12.2 us
    all_to_all x1, starting transfers between devices, body(): received = lax.all_to_all(blocks, ('member', 'space'), 0, 0, tiled=True)  11.1 us
    ppermute x1, waiting for transfers between devices, body(): b_temp = lax.ppermute(b_temp, 'space', across)  8.61 us
    all_to_all x1, starting transfers between devices, body(): tiles = lax.all_to_all(tiles, 'space', 0, 0, tiled=True)  5.27 us
    ppermute x1, starting transfers between devices, body(): b_cot = lax.ppermute(b_cot, 'space', across)  4.76 us
    ppermute x1, starting transfers between devices, body(): b_temp = lax.ppermute(b_temp, 'space', across)  4.12 us
    pallas_call x1, Pallas kernels, body(): pl.pallas_call(pack_kernel, out_shape=(shape(planes + 1, HALO, cols), sha...  3.21 us
  transfers between devices with their start and end apart: 6, of which 2 were waited for; matrix products, arithmetic and copies ran while one was open for 0% of the time, Pallas kernels for 35%

profile of v1, /device:TPU:1, one launch (start us, length us, event | category | flops | bytes accessed | tf_op | source)
XLA Modules:
  0.0 69.9 jit_solution(16950077968118549774)
XLA Ops:
  0.6 3.2 %pack.1 = (f32[21,4,640]{2,1,0:T(4,128)}, f32[21,4,640]{2,1,0:T(4,128)}, f32[22,4,640]{2,1,0:T(4,128)}, f32[22,4,640]{2,1,0:T(4,128)}, f32[16,8,128]{2,1,0:T(8,128)}) custom-call(f32[2,10,40,640]{3,2,1,0:T(8,128)} %cot.3, f32[2,10,40,640]{3,2,1,0:T(8,128)} %temp.3, f32[2,40,640]{2,1,0:T(8,128)} %forcing.3, s32[40,640]{1,0:T(8,128)} %soil.5, f32[10,2,32]{2,1,0:T(2,128)} %parent.1), custom_call_target="tpu_custom_call" | custom-call | tf_op jit(solution)/shard_map/pack/pallas_call | solution.py:305
  3.8 0.0 copy-start.7
  3.9 1.5 %collective-permute-start.2 = (f32[21,4,640]{2,1,0:T(4,128)}, f32[21,4,640]{2,1,0:T(4,128)S(1)}, u32[]{:S(2)}, u32[]{:S(2)}) collective-permute-start(f32[21,4,640]{2,1,0:T(4,128)} %get-tuple-element.12), channel_id=1, source_target_pairs={{0,8},{8,0},{16,24},{24,16},{32,40},{40,32},{48,56},{56,48},{64,72... | collective-permute-start | bytes 645128 | tf_op jit(solution)/shard_map/ppermute | solution.py:323
  5.4 4.8 %collective-permute-start.3 = (f32[21,4,640]{2,1,0:T(4,128)}, f32[21,4,640]{2,1,0:T(4,128)S(1)}, u32[]{:S(2)}, u32[]{:S(2)}) collective-permute-start(f32[21,4,640]{2,1,0:T(4,128)} %get-tuple-element.13), channel_id=1, source_target_pairs={{8,16},{24,32},{40,48},{56,64},{72,80},{88,96},{104,112},{16,8},{3... | collective-permute-start | bytes 645128 | tf_op jit(solution)/shard_map/ppermute | solution.py:324
  10.1 5.3 %all-to-all-start = ((f32[16,8,128]{2,1,0:T(8,128)}), f32[16,8,128]{2,1,0:T(8,128)S(1)}, u32[]{:S(2)}, u32[]{:S(2)}) async-start(f32[16,8,128]{2,1,0:T(8,128)} %get-tuple-element.14), calls=%async_computation | async-start | bytes 131072 | tf_op jit(solution)/shard_map/all_to_all | solution.py:327
  15.4 0.0 collective-permute-done.2.a_cot
  15.4 0.0 copy-start.1
  15.4 0.6 collective-permute-done.3.b_cot
  16.1 0.1 copy-done.1
  16.1 0.7 copy-done.2
  16.8 12.2 %adjoint.1 = (f32[2,10,40,640]{3,2,1,0:T(8,128)}, f32[128,8,128]{2,1,0:T(8,128)}) custom-call(f32[2,10,40,640]{3,2,1,0:T(8,128)} %cot.3, f32[21,4,640]{2,1,0:T(4,128)} %copy-done.1, f32[21,4,640]{2,1,0:T(4,128)} %copy-done.2, s32[40,640]{1,0:T(8,128)} %soil.5, f32[12,10]{1,0:T(8,128)} %cond.3, s32[16]{0:T(128)} %tile_map.3), custom_call_target="tpu_custom_call" | custom-call | flops 36864000 | bytes 4096000 | tf_op jit(solution)/shard_map/adjoint/pallas_call | solution.py:330
  29.0 0.0 all-to-all-done.tiles
  29.0 11.1 %all-to-all-start.1 = ((f32[128,8,128]{2,1,0:T(8,128)}), f32[128,8,128]{2,1,0:T(8,128)S(1)}, u32[]{:S(2)}, u32[]{:S(2)}) async-start(f32[128,8,128]{2,1,0:T(8,128)} %get-tuple-element.16), calls=%async_computation.1 | async-start | bytes 1048576 | tf_op jit(solution)/shard_map/all_to_all | solution.py:348
  40.2 1.1 %collective-permute-start = (f32[22,4,640]{2,1,0:T(4,128)S(1)}, f32[22,4,640]{2,1,0:T(4,128)S(1)}, u32[]{:S(2)}, u32[]{:S(2)}) collective-permute-start(f32[22,4,640]{2,1,0:T(4,128)S(1)} %copy-done.7), channel_id=1, source_target_pairs={{0,8},{8,0},{16,24},{24,16},{32,40},{40,32},{48,56},{56,48},{64,72... | collective-permute-start | bytes 675848 | tf_op jit(solution)/shard_map/ppermute | solution.py:325
  41.3 0.0 copy-done.6
  41.3 4.1 %collective-permute-start.1 = (f32[22,4,640]{2,1,0:T(4,128)S(1)}, f32[22,4,640]{2,1,0:T(4,128)S(1)}, u32[]{:S(2)}, u32[]{:S(2)}) collective-permute-start(f32[22,4,640]{2,1,0:T(4,128)S(1)} %copy-done.6), channel_id=1, source_target_pairs={{8,16},{24,32},{40,48},{56,64},{72,80},{88,96},{104,112},{16,8},{3... | collective-permute-start | bytes 675848 | tf_op jit(solution)/shard_map/ppermute | solution.py:326
  45.4 0.0 collective-permute-done.a_temp
  45.5 8.6 %collective-permute-done.1.b_temp = f32[22,4,640]{2,1,0:T(4,128)S(1)} collective-permute-done((f32[22,4,640]{2,1,0:T(4,128)S(1)}, f32[22,4,640]{2,1,0:T(4,128)S(1)}, u32[]{:S(2)}, u32[]{:S(2)}) %collective-permute-start.1) | collective-permute-done | bytes 225312 | tf_op jit(solution)/shard_map/ppermute | solution.py:326
  54.1 0.0 copy-done.3
  54.1 0.7 copy-done.5
  54.8 12.4 %forward.1 = f32[2,10,40,640]{3,2,1,0:T(8,128)} custom-call(f32[2,10,40,640]{3,2,1,0:T(8,128)} %temp.3, f32[2,40,640]{2,1,0:T(8,128)} %forcing.3, f32[22,4,640]{2,1,0:T(4,128)} %copy-done.4, f32[22,4,640]{2,1,0:T(4,128)} %copy-done.5, f32[21,4,640]{2,1,0:T(4,128)} %copy-done.1, f32[21,4,640]{2,1,0:T(4,128)} %copy-done.2, s32[40,640]{1,0:T(8,128)} %soil.5, ...), custom_call_target="tpu_custom_call" | custom-call | flops 36864000 | bytes 4096000 | tf_op jit(solution)/shard_map/forward/pallas_call | solution.py:349
  67.2 0.0 all-to-all-done.1.received
  67.2 0.8 %copy-done = f32[128,8,128]{2,1,0:T(8,128)} copy-done((f32[128,8,128]{2,1,0:T(8,128)}, f32[128,8,128]{2,1,0:T(8,128)S(1)}, u32[]{:S(2)}) %copy-start) | copy-done | bytes 524312
  68.0 1.9 %collect.1 = f32[10,2,32]{2,1,0:T(2,128)} custom-call(f32[128,8,128]{2,1,0:T(8,128)} %copy-done), custom_call_target="tpu_custom_call" | custom-call | tf_op jit(solution)/shard_map/collect/pallas_call | solution.py:367
  (8 shorter events, 0.0 us)
Async XLA Ops:
  3.8 36.3 %copy-start.7 = (f32[22,4,640]{2,1,0:T(4,128)S(1)}, f32[22,4,640]{2,1,0:T(4,128)}, u32[]{:S(2)}) copy-start(f32[22,4,640]{2,1,0:T(4,128)} %get-tuple-element.10) | copy-start | bytes 675844
  3.9 37.5 %copy-start.6 = (f32[22,4,640]{2,1,0:T(4,128)S(1)}, f32[22,4,640]{2,1,0:T(4,128)}, u32[]{:S(2)}) copy-start(f32[22,4,640]{2,1,0:T(4,128)} %get-tuple-element.11) | copy-start | bytes 675844
  3.9 11.6 %collective-permute-start.2 = (f32[21,4,640]{2,1,0:T(4,128)}, f32[21,4,640]{2,1,0:T(4,128)S(1)}, u32[]{:S(2)}, u32[]{:S(2)}) collective-permute-start(f32[21,4,640]{2,1,0:T(4,128)} %get-tuple-element.12), channel_id=1, source_target_pairs={{0,8},{8,0},{16,24},{24,16},{32,40},{40,32},{48,56},{56,48},{64,72... | collective-permute-start | bytes 645128 | tf_op jit(solution)/shard_map/ppermute | solution.py:323
  5.4 10.7 %collective-permute-start.3 = (f32[21,4,640]{2,1,0:T(4,128)}, f32[21,4,640]{2,1,0:T(4,128)S(1)}, u32[]{:S(2)}, u32[]{:S(2)}) collective-permute-start(f32[21,4,640]{2,1,0:T(4,128)} %get-tuple-element.13), channel_id=1, source_target_pairs={{8,16},{24,32},{40,48},{56,64},{72,80},{88,96},{104,112},{16,8},{3... | collective-permute-start | bytes 645128 | tf_op jit(solution)/shard_map/ppermute | solution.py:324
  10.1 18.9 %all-to-all-start = ((f32[16,8,128]{2,1,0:T(8,128)}), f32[16,8,128]{2,1,0:T(8,128)S(1)}, u32[]{:S(2)}, u32[]{:S(2)}) async-start(f32[16,8,128]{2,1,0:T(8,128)} %get-tuple-element.14), calls=%async_computation | async-start | bytes 131072 | tf_op jit(solution)/shard_map/all_to_all | solution.py:327
  15.4 0.7 %copy-start.1 = (f32[21,4,640]{2,1,0:T(4,128)}, f32[21,4,640]{2,1,0:T(4,128)S(1)}, u32[]{:S(2)}) copy-start(f32[21,4,640]{2,1,0:T(4,128)S(1)} %collective-permute-done.2.a_cot) | copy-start | bytes 645124
  16.1 0.7 %copy-start.2 = (f32[21,4,640]{2,1,0:T(4,128)}, f32[21,4,640]{2,1,0:T(4,128)S(1)}, u32[]{:S(2)}) copy-start(f32[21,4,640]{2,1,0:T(4,128)S(1)} %collective-permute-done.3.b_cot) | copy-start | bytes 645124
  29.0 25.1 %copy-start.3 = (f32[16,8,128]{2,1,0:T(8,128)}, f32[16,8,128]{2,1,0:T(8,128)S(1)}, u32[]{:S(2)}) copy-start(f32[16,8,128]{2,1,0:T(8,128)S(1)} %all-to-all-done.tiles) | copy-start | bytes 196612
  29.0 38.2 %all-to-all-start.1 = ((f32[128,8,128]{2,1,0:T(8,128)}), f32[128,8,128]{2,1,0:T(8,128)S(1)}, u32[]{:S(2)}, u32[]{:S(2)}) async-start(f32[128,8,128]{2,1,0:T(8,128)} %get-tuple-element.16), calls=%async_computation.1 | async-start | bytes 1048576 | tf_op jit(solution)/shard_map/all_to_all | solution.py:348
  40.2 5.3 %collective-permute-start = (f32[22,4,640]{2,1,0:T(4,128)S(1)}, f32[22,4,640]{2,1,0:T(4,128)S(1)}, u32[]{:S(2)}, u32[]{:S(2)}) collective-permute-start(f32[22,4,640]{2,1,0:T(4,128)S(1)} %copy-done.7), channel_id=1, source_target_pairs={{0,8},{8,0},{16,24},{24,16},{32,40},{40,32},{48,56},{56,48},{64,72... | collective-permute-start | bytes 675848 | tf_op jit(solution)/shard_map/ppermute | solution.py:325
  41.3 12.8 %collective-permute-start.1 = (f32[22,4,640]{2,1,0:T(4,128)S(1)}, f32[22,4,640]{2,1,0:T(4,128)S(1)}, u32[]{:S(2)}, u32[]{:S(2)}) collective-permute-start(f32[22,4,640]{2,1,0:T(4,128)S(1)} %copy-done.6), channel_id=1, source_target_pairs={{8,16},{24,32},{40,48},{56,64},{72,80},{88,96},{104,112},{16,8},{3... | collective-permute-start | bytes 675848 | tf_op jit(solution)/shard_map/ppermute | solution.py:326
  45.5 8.6 %copy-start.4 = (f32[22,4,640]{2,1,0:T(4,128)}, f32[22,4,640]{2,1,0:T(4,128)S(1)}, u32[]{:S(2)}) copy-start(f32[22,4,640]{2,1,0:T(4,128)S(1)} %collective-permute-done.a_temp) | copy-start | bytes 675844
  54.1 0.7 copy-start.5
  67.2 0.8 %copy-start = (f32[128,8,128]{2,1,0:T(8,128)}, f32[128,8,128]{2,1,0:T(8,128)S(1)}, u32[]{:S(2)}) copy-start(f32[128,8,128]{2,1,0:T(8,128)S(1)} %all-to-all-done.1.received) | copy-start | bytes 1572868

commit v2 on v1

--- a/solution.py
+++ b/solution.py
@@ -20,7 +20,16 @@
 VM = pl.BlockSpec(memory_space=pltpu.VMEM)
 SM = pl.BlockSpec(memory_space=pltpu.SMEM)
 HB = pl.BlockSpec(memory_space=pl.ANY)
-PARAMS = pltpu.CompilerParams(vmem_limit_bytes=56 * 1024 * 1024)
+SMALL = pltpu.CompilerParams(vmem_limit_bytes=6 * 1024 * 1024)
+PARAMS = pltpu.CompilerParams(vmem_limit_bytes=24 * 1024 * 1024)
+
+
+def far(x):
+    return pltpu.with_memory_space_constraint(x, pltpu.HBM)
+
+
+def near(x):
+    return pltpu.with_memory_space_constraint(x, pltpu.VMEM)
 
 
 def cols_of(c):
@@ -33,43 +42,65 @@
     return (y // rows + 32 * group == lane).astype(f32)
 
 
-def pack_kernel(cot, temp, forcing, soil, parent, a_cot, b_cot, a_temp, b_temp, tiles, edge_c, edge_t, edge_f, edge_s, flat, sems):
-    rows = cot.shape[2]
-    odd = lax.axis_index("space") % 2
-    copies = []
-    for side, start in ((0, 0), (1, rows - 8)):
-        cut = pl.ds(start, 8)
-        copies.append(pltpu.make_async_copy(cot.at[:, :, cut, :], edge_c.at[side], sems.at[side, 0]))
-        copies.append(pltpu.make_async_copy(soil.at[cut, :], edge_s.at[side], sems.at[side, 1]))
-        copies.append(pltpu.make_async_copy(temp.at[:, :, cut, :], edge_t.at[side], sems.at[side, 2]))
-        copies.append(pltpu.make_async_copy(forcing.at[:, cut, :], edge_f.at[side], sems.at[side, 3]))
+def send_rows(odd, pieces):
+    for parity in (0, 1):
+        @pl.when(odd == parity)
+        def _():
+            for take, plane, near_msg, far_msg in pieces:
+                low, high = take(True), take(False)
+                first, second = (far_msg, near_msg) if parity == 0 else (near_msg, far_msg)
+                first[plane] = low()
+                second[plane] = high()
+
+
+def taker(ref, *index, convert=None):
+    def take(top):
+        def get():
+            value = ref[(0 if top else 1, *index, slice(0, HALO) if top else slice(8 - HALO, 8), slice(None))]
+            return convert(value) if convert else value
+
+        return get
+
+    return take
+
+
+def edge_copies(pairs, rows, sems):
+    out = []
+    for n, (field, edges) in enumerate(pairs):
+        for side, start in ((0, 0), (1, rows - 8)):
+            cut = (*[slice(None)] * (len(field.shape) - 2), pl.ds(start, 8), slice(None))
+            out.append(pltpu.make_async_copy(field.at[cut], edges.at[side], sems.at[n, side]))
+    return out
+
+
+def pack_kernel(cot, temp, forcing, soil, parent, a_msg, b_msg, tiles, flat, edge_c, edge_t, edge_f, edge_s, held, sems, sem):
+    members, layers, rows = cot.shape[:3]
+    get_parent = pltpu.make_async_copy(parent, held, sem)
+    get_parent.start()
+    copies = edge_copies(((cot, edge_c), (temp, edge_t), (forcing, edge_f), (soil, edge_s)), rows, sems)
     for copy in copies:
         copy.start()
-    members, layers = cot.shape[:2]
-    groups = -(-2 * layers // 8)
+    odd = lax.axis_index("space") % 2
     flat[...] = jnp.zeros_like(flat)
+    get_parent.wait()
     for l in range(layers):
-        flat[2 * l:2 * l + 2, :] = parent[l]
+        flat[2 * l:2 * l + 2, :] = held[l]
     packed = jnp.zeros((8, LANES), f32)
-    for g in range(groups):
+    for g in range(flat.shape[0] // 8):
         packed = packed + jnp.dot(flat[8 * g:8 * g + 8, :], spread(g, 1, flat.shape[1]), precision=HIGHEST)
     for i in range(tiles.shape[0]):
         tiles[i] = packed
     for copy in copies:
         copy.wait()
-    for parity in (0, 1):
-        @pl.when(odd == parity)
-        def _():
-            low, high = (slice(0, 4), slice(4, 8))
-            for side, cut in ((0, low), (1, high)):
-                to_a = (side == 1) == (parity == 0)
-                oc, ot = (a_cot, a_temp) if to_a else (b_cot, b_temp)
-                for m in range(members):
-                    for l in range(layers):
-                        oc[m * layers + l] = edge_c[side, m, l, cut, :]
-                        ot[m * layers + l] = edge_t[side, m, l, cut, :]
-                    ot[members * layers + m] = edge_f[side, m, cut, :]
-                oc[members * layers] = edge_s[side, cut, :].astype(f32) + 1.0
+    planes = members * layers
+    pieces = []
+    for m in range(members):
+        for l in range(layers):
+            pieces.append((taker(edge_c, m, l), m * layers + l, a_msg, b_msg))
+            pieces.append((taker(edge_t, m, l), planes + m * layers + l, a_msg, b_msg))
+        pieces.append((taker(edge_f, m), 2 * planes + m, a_msg, b_msg))
+    pieces.append((taker(edge_s, convert=lambda v: v.astype(f32) + 1.0), 2 * planes + members, a_msg, b_msg))
+    send_rows(odd, pieces)
 
 
 def side_rows(odd, a_ref, b_ref, p):
@@ -77,9 +108,9 @@
     return jnp.where(odd == 1, a, b), jnp.where(odd == 1, b, a)
 
 
-def fill_kappa(soil, a_cot, b_cot, cond, odd, layers, S, K, C):
+def fill_kappa(soil, a_msg, b_msg, cond, odd, layers, S, K, C):
     rows, cols = soil.shape
-    top, bottom = side_rows(odd, a_cot, b_cot, a_cot.shape[0] - 1)
+    top, bottom = side_rows(odd, a_msg, b_msg, a_msg.shape[0] - 1)
     lane = lax.broadcasted_iota(jnp.int32, (8, LANES), 1)
     for c in range(cols // LANES):
         S[c, 0:HALO, :] = top[:, cols_of(c)].astype(jnp.int32) - 1
@@ -100,11 +131,11 @@
                 C[l, c, cut, :] = KEEP - 4.0 * kappa
 
 
-def fill_field(field, a_ref, b_ref, odd, X):
+def fill_field(field, a_ref, b_ref, odd, X, first):
     members, layers, rows, cols = field.shape
 
     def plane(p, carry):
-        top, bottom = side_rows(odd, a_ref, b_ref, p)
+        top, bottom = side_rows(odd, a_ref, b_ref, first + p)
         for c in range(cols // LANES):
             X[0, p, c, 0:HALO, :] = top[:, cols_of(c)]
             X[0, p, c, rows + HALO:, :] = bottom[:, cols_of(c)]
@@ -131,14 +162,20 @@
     return jnp.minimum(1 + 8 * i, rows + 2 * HALO - 9)
 
 
-def adjoint_kernel(cot, a_cot, b_cot, soil, cond, tile_map, adj, blocks, X, W, K, C, S, RS, BS):
+def row_copy(src, dst, sems, i):
+    cut = pl.ds(pl.multiple_of(8 * i, 8), 8)
+    return pltpu.make_async_copy(src.at[:, :, cut, :], dst.at[:, :, cut, :], sems.at[i])
+
+
+def adjoint_kernel(cot, a_msg, b_msg, soil, cond, tile_map, adj_out, blocks_out, X, W, K, C, S, RS, BS, blocks, adj, sems, sem):
     members, layers, rows, cols = cot.shape
     position = lax.axis_index("space")
     odd = position % 2
     nb = cols // LANES
     chunks = RS.shape[0]
-    fill_kappa(soil, a_cot, b_cot, cond, odd, layers, S, K, C)
-    fill_field(cot, a_cot, b_cot, odd, X)
+    send_blocks = pltpu.make_async_copy(blocks, blocks_out, sem.at[0])
+    fill_kappa(soil, a_msg, b_msg, cond, odd, layers, S, K, C)
+    fill_field(cot, a_msg, b_msg, odd, X, 0)
 
     def weigh(p, carry):
         for c in range(nb):
@@ -180,9 +217,11 @@
                     for c in range(nb):
                         RS[i, l, c] = total[c] if k == 0 else RS[i, l, c] + total[c]
                 above, here = here, after
+            if last:
+                row_copy(adj, adj_out, sems, i).start()
             return carry
 
-        lax.fori_loop(0, rows // 8 if last else chunks, chunk, 0)
+        lax.fori_loop(0, rows // 8 if last else chunks, chunk, 0, unroll=True)
         if k == ITERS - 2:
             row = lax.broadcasted_iota(jnp.int32, (8, LANES), 0)
             BS[...] = jnp.zeros_like(BS)
@@ -212,17 +251,24 @@
             owner = tile_map[position]
             for m in range(blocks.shape[0] // spaces):
                 blocks[m * spaces + owner] = packed
-
-
-def forward_kernel(temp, forcing, a_temp, b_temp, a_cot, b_cot, soil, cond, tiles, tile_map, out, X, K, C, S, T, F, TE):
+            send_blocks.start()
+    for i in range(rows // 8):
+        row_copy(adj, adj_out, sems, i).wait()
+    send_blocks.wait()
+
+
+def forward_kernel(temp, forcing_in, a_msg, b_msg, soil, cond, tiles, tile_map, result, X, K, C, S, T, F, TE, out, forcing, sems, sem):
+    get_temp = pltpu.make_async_copy(temp, out, sem.at[0])
+    get_forcing = pltpu.make_async_copy(forcing_in, forcing, sem.at[1])
+    get_temp.start()
+    get_forcing.start()
     members, layers, rows, cols = temp.shape
     spaces = tile_map.shape[0]
     position = lax.axis_index("space")
     odd = position % 2
     nb = cols // LANES
     ext = rows + 2 * HALO
-    fill_kappa(soil, a_cot, b_cot, cond, odd, layers, S, K, C)
-    fill_field(temp, a_temp, b_temp, odd, X)
+    fill_kappa(soil, a_msg, b_msg, cond, odd, layers, S, K, C)
     around = []
     for shift in (-1, 0, 1):
         where = jnp.minimum(jnp.maximum(position + shift, 0), spaces - 1)
@@ -243,8 +289,11 @@
         for c in range(nb):
             for lo, hi, value in bands:
                 T[l, c, lo:hi, :] = jnp.broadcast_to(value[:, cols_of(c)], (hi - lo, LANES))
+    get_temp.wait()
+    fill_field(out, a_msg, b_msg, odd, X, members * layers)
+    get_forcing.wait()
     for m in range(members):
-        top, bottom = side_rows(odd, a_temp, b_temp, members * layers + m)
+        top, bottom = side_rows(odd, a_msg, b_msg, 2 * members * layers + m)
         for c in range(nb):
             F[m, c, 0:HALO, :] = T[0, c, 0:HALO, :] + top[:, cols_of(c)]
             F[m, c, rows + HALO:, :] = T[0, c, rows + HALO:, :] + bottom[:, cols_of(c)]
@@ -275,9 +324,13 @@
                         else:
                             X[dst, p, c, mid, :] = new
                 above, here = here, after
+            if last:
+                row_copy(out, result, sems, i).start()
             return carry
 
-        lax.fori_loop(0, rows // 8 if last else -(-(ext - 2) // 8), chunk, 0)
+        lax.fori_loop(0, rows // 8 if last else -(-(ext - 2) // 8), chunk, 0, unroll=True)
+    for i in range(rows // 8):
+        row_copy(out, result, sems, i).wait()
 
 
 def sum_kernel(received, out, total):
@@ -302,36 +355,42 @@
     chunks = -(-(ext - 2) // 8)
     pieces = -(-2 * layers // 8)
     shape = lambda *dims: jax.ShapeDtypeStruct(dims, f32)
-    a_cot, b_cot, a_temp, b_temp, tiles = pl.pallas_call(
+    local = lambda *dims: pltpu.VMEM(dims, f32)
+    edges = lambda kind, *dims: pltpu.VMEM((2, *dims, 8, cols), kind)
+    total = 2 * planes + members + 1
+    a_msg, b_msg, tiles = pl.pallas_call(
         pack_kernel,
-        out_shape=(shape(planes + 1, HALO, cols), shape(planes + 1, HALO, cols), shape(planes + members, HALO, cols), shape(planes + members, HALO, cols), shape(spaces, 8, LANES)),
-        in_specs=[HB, HB, HB, HB, VM],
-        out_specs=[VM] * 5,
+        out_shape=(shape(total, HALO, cols), shape(total, HALO, cols), shape(spaces, 8, LANES)),
+        in_specs=[HB] * 5,
+        out_specs=[VM] * 3,
         scratch_shapes=[
-            pltpu.VMEM((2, members, layers, 8, cols), f32),
-            pltpu.VMEM((2, members, layers, 8, cols), f32),
-            pltpu.VMEM((2, members, 8, cols), f32),
-            pltpu.VMEM((2, 8, cols), jnp.int32),
             pltpu.VMEM((8 * pieces, parent_field.shape[2]), f32),
-            pltpu.SemaphoreType.DMA((2, 4)),
+            edges(f32, members, layers),
+            edges(f32, members, layers),
+            edges(f32, members),
+            edges(jnp.int32),
+            pltpu.VMEM(parent_field.shape, f32),
+            pltpu.SemaphoreType.DMA((4, 2)),
+            pltpu.SemaphoreType.DMA,
         ],
-        compiler_params=PARAMS,
+        compiler_params=SMALL,
         name="pack",
-    )(cotangent, temp_start, forcing, soil_class, parent_field)
+    )(far(cotangent), far(temp_start), far(forcing), far(soil_class), far(parent_field))
     pair = [(i, i ^ 1) for i in range(spaces)]
     across = [(i, i + 1) for i in range(1, spaces - 1, 2)] + [(i + 1, i) for i in range(1, spaces - 1, 2)]
-    a_cot = lax.ppermute(a_cot, "space", pair)
-    b_cot = lax.ppermute(b_cot, "space", across)
-    a_temp = lax.ppermute(a_temp, "space", pair)
-    b_temp = lax.ppermute(b_temp, "space", across)
+    a_msg = near(lax.ppermute(a_msg, "space", pair))
+    b_msg = near(lax.ppermute(b_msg, "space", across))
     tiles = lax.all_to_all(tiles, "space", 0, 0, tiled=True)
     flops = 15 * planes * ext * cols * ITERS
     cost = pl.CostEstimate(flops=flops, bytes_accessed=4 * 2 * planes * rows * cols, transcendentals=0)
     adjoint, blocks = pl.pallas_call(
         adjoint_kernel,
-        out_shape=(jax.ShapeDtypeStruct(cotangent.shape, f32), shape(groups * spaces, 8, LANES)),
+        out_shape=(
+            shape(*cotangent.shape),
+            shape(groups * spaces, 8, LANES),
+        ),
         in_specs=[VM, VM, VM, VM, SM, SM],
-        out_specs=[VM, VM],
+        out_specs=[HB, HB],
         scratch_shapes=[
             pltpu.VMEM((2, planes, nb, ext, LANES), f32),
             pltpu.VMEM((2, planes, nb, ext, LANES), f32),
@@ -340,17 +399,22 @@
             pltpu.VMEM((nb, ext, LANES), jnp.int32),
             pltpu.VMEM((chunks, layers, nb, 8, LANES), f32),
             pltpu.VMEM((8 * pieces, cols), f32),
+            pltpu.VMEM((groups * spaces, 8, LANES), f32),
+            pltpu.VMEM(cotangent.shape, f32),
+            pltpu.SemaphoreType.DMA((rows // 8,)),
+            pltpu.SemaphoreType.DMA((1,)),
         ],
         compiler_params=PARAMS,
         cost_estimate=cost,
         name="adjoint",
-    )(cotangent, a_cot, b_cot, soil_class, conductivity, tile_map)
+    )(near(cotangent), a_msg, b_msg, near(soil_class), conductivity, tile_map)
+    blocks, tiles = lax.optimization_barrier((blocks, tiles))
     received = lax.all_to_all(blocks, ("member", "space"), 0, 0, tiled=True)
-    temp = pl.pallas_call(
+    final = pl.pallas_call(
         forward_kernel,
-        out_shape=jax.ShapeDtypeStruct(temp_start.shape, f32),
-        in_specs=[VM, VM, VM, VM, VM, VM, VM, SM, VM, SM],
-        out_specs=VM,
+        out_shape=shape(*temp_start.shape),
+        in_specs=[HB, HB] + [VM] * 3 + [SM, VM, SM],
+        out_specs=HB,
         scratch_shapes=[
             pltpu.VMEM((2, planes, nb, ext, LANES), f32),
             pltpu.VMEM((layers, nb, ext, LANES), f32),
@@ -359,21 +423,25 @@
             pltpu.VMEM((layers, nb, ext, LANES), f32),
             pltpu.VMEM((members, nb, ext, LANES), f32),
             pltpu.VMEM((pieces, 24, cols), f32),
+            pltpu.VMEM(temp_start.shape, f32),
+            pltpu.VMEM(forcing.shape, f32),
+            pltpu.SemaphoreType.DMA((rows // 8,)),
+            pltpu.SemaphoreType.DMA((2,)),
         ],
         compiler_params=PARAMS,
         cost_estimate=cost,
         name="forward",
-    )(temp_start, forcing, a_temp, b_temp, a_cot, b_cot, soil_class, conductivity, tiles, tile_map)
+    )(far(temp_start), far(forcing), a_msg, b_msg, near(soil_class), conductivity, tiles, tile_map)
     parent_grad = pl.pallas_call(
         sum_kernel,
-        out_shape=shape(*parent_field.shape),
+        out_shape=jax.ShapeDtypeStruct(parent_field.shape, f32),
         in_specs=[VM],
         out_specs=VM,
         scratch_shapes=[pltpu.VMEM((8, LANES), f32)],
         compiler_params=PARAMS,
         name="collect",
-    )(received)
-    return temp, adjoint, parent_grad
+    )(near(received))
+    return final, adjoint, parent_grad
 
 
 def solution(mesh):

time: 70.3 us -> 55.9 us (0.80)
  Pallas kernels: 29.7 us -> 21.8 us
  starting transfers between devices: 27.9 us -> 22.1 us
  local copies, waits for them, and re-layouts: 2.25 us -> 0.81 us
  waiting for transfers between devices: 9.26 us -> 10.2 us
    pallas_call x4, Pallas kernels: 29.7 us -> 21.8 us  [the longest x1 9.22 us: body(): pl.pallas_call(forward_kernel, out_shape=shape(*temp_start.shape), in_spe...]
    ppermute x4 -> x2, starting transfers between devices: 11.5 us -> 6.14 us  [the longest x1 4.63 us: body(): b_msg = near(lax.ppermute(b_msg, 'space', across))]
    all_to_all x1, waiting for transfers between devices: 0.01 us -> 4.38 us  [body(): received = lax.all_to_all(blocks, ('member', 'space'), 0, 0, tiled=True)]
    ppermute x4 -> x2, waiting for transfers between devices: 9.25 us -> 5.84 us  [the longest x1 5.84 us: body(): b_msg = near(lax.ppermute(b_msg, 'space', across))]
    unnamed x16 -> x10, local copies, waits for them, and re-layouts: 2.25 us -> 0.81 us
  transfers between devices with their start and end apart: 6 -> 4, of which waited for: 2 -> 2; matrix products, arithmetic and copies ran while one was open for 0% -> 0% of each run, Pallas kernels for 35% -> 33%
where the time goes in v2:
time: 55.9 us; the launch traced here: 55.6 us
  starting transfers between devices  22.1 us (40%)
  Pallas kernels  21.8 us (39%)
  waiting for transfers between devices  10.2 us (18%)
  local copies, waits for them, and re-layouts  0.81 us (1%)
  between operations  0.73 us (1%)
    all_to_all x1, starting transfers between devices, body(): received = lax.all_to_all(blocks, ('member', 'space'), 0, 0, tiled=True)  10.7 us
    pallas_call x1, Pallas kernels, body(): pl.pallas_call(forward_kernel, out_shape=shape(*temp_start.shape), in_spe...  9.22 us
    pallas_call x1, Pallas kernels, body(): pl.pallas_call(adjoint_kernel, out_shape=(shape(*cotangent.shape), shape(...  9.19 us
    ppermute x1, waiting for transfers between devices, body(): b_msg = near(lax.ppermute(b_msg, 'space', across))  5.84 us
    all_to_all x1, starting transfers between devices, body(): tiles = lax.all_to_all(tiles, 'space', 0, 0, tiled=True)  5.27 us
    ppermute x1, starting transfers between devices, body(): b_msg = near(lax.ppermute(b_msg, 'space', across))  4.63 us
    all_to_all x1, waiting for transfers between devices, body(): received = lax.all_to_all(blocks, ('member', 'space'), 0, 0, tiled=True)  4.38 us
    pallas_call x1, Pallas kernels, body(): pl.pallas_call(pack_kernel, out_shape=(shape(total, HALO, cols), shape(to...  2.52 us
  transfers between devices with their start and end apart: 4, of which 2 were waited for; matrix products, arithmetic and copies ran while one was open for 0% of the time, Pallas kernels for 33%

profile of v2, /device:TPU:1, one launch (start us, length us, event | category | flops | bytes accessed | tf_op | source)
XLA Modules:
  0.0 55.6 jit_solution(4883857258939181561)
XLA Ops:
  0.6 0.0 copy-start.1
  0.6 0.0 copy-start
  0.7 0.0 copy-start.4
  0.7 0.0 copy-start.3
  0.7 2.5 %pack.1 = (f32[43,4,640]{2,1,0:T(4,128)}, f32[43,4,640]{2,1,0:T(4,128)S(1)}, f32[16,8,128]{2,1,0:T(8,128)}) custom-call(f32[2,10,40,640]{3,2,1,0:T(8,128)} %cot.3, f32[2,10,40,640]{3,2,1,0:T(8,128)} %temp.3, f32[2,40,640]{2,1,0:T(8,128)} %forcing_in.1, s32[40,640]{1,0:T(8,128)} %soil.5, f32[10,2,32]{2,1,0:T(2,128)} %parent.1), custom_call_target="tpu_custom_call" | custom-call | tf_op jit(solution)/shard_map/pack/pallas_call | solution.py:361
  3.2 1.5 %collective-permute-start = (f32[43,4,640]{2,1,0:T(4,128)}, f32[43,4,640]{2,1,0:T(4,128)S(1)}, u32[]{:S(2)}, u32[]{:S(2)}) collective-permute-start(f32[43,4,640]{2,1,0:T(4,128)} %get-tuple-element.10), channel_id=1, source_target_pairs={{0,8},{8,0},{16,24},{24,16},{32,40},{40,32},{48,56},{56,48},{64,72... | collective-permute-start | bytes 1320968 | tf_op jit(solution)/shard_map/ppermute | solution.py:381
  4.7 4.6 %collective-permute-start.1 = (f32[43,4,640]{2,1,0:T(4,128)S(1)}, f32[43,4,640]{2,1,0:T(4,128)S(1)}, u32[]{:S(2)}, u32[]{:S(2)}) collective-permute-start(f32[43,4,640]{2,1,0:T(4,128)S(1)} %get-tuple-element.11), channel_id=1, source_target_pairs={{8,16},{24,32},{40,48},{56,64},{72,80},{88,96},{104,112},{16,8},{3... | collective-permute-start | bytes 1320968 | tf_op jit(solution)/shard_map/ppermute | solution.py:382
  9.3 5.3 %all-to-all-start = ((f32[16,8,128]{2,1,0:T(8,128)}), f32[16,8,128]{2,1,0:T(8,128)S(1)}, u32[]{:S(2)}, u32[]{:S(2)}) async-start(f32[16,8,128]{2,1,0:T(8,128)} %get-tuple-element.13), calls=%async_computation | async-start | bytes 131072 | tf_op jit(solution)/shard_map/all_to_all | solution.py:383
  14.6 0.0 collective-permute-done.a_msg
  14.6 5.8 %collective-permute-done.1.b_msg = f32[43,4,640]{2,1,0:T(4,128)S(1)} collective-permute-done((f32[43,4,640]{2,1,0:T(4,128)S(1)}, f32[43,4,640]{2,1,0:T(4,128)S(1)}, u32[]{:S(2)}, u32[]{:S(2)}) %collective-permute-start.1) | collective-permute-done | bytes 440352 | tf_op jit(solution)/shard_map/ppermute | solution.py:382
  20.5 0.0 copy-done.1
  20.5 0.0 copy-done
  20.5 0.0 copy-done.4
  20.5 0.0 copy-done.3
  20.5 9.2 %adjoint.1 = (f32[2,10,40,640]{3,2,1,0:T(8,128)}, f32[128,8,128]{2,1,0:T(8,128)S(1)}) custom-call(f32[2,10,40,640]{3,2,1,0:T(8,128)S(1)} %copy-done, f32[43,4,640]{2,1,0:T(4,128)S(1)} %collective-permute-done.a_msg, f32[43,4,640]{2,1,0:T(4,128)S(1)} %collective-permute-done.1.b_msg, s32[40,640]{1,0:T(8,128)S(1)} %copy-done.1, f32[12,10]{1,0:T(8,128)S(1)} %copy-done.3, ...), custom_call_target="tpu_custom_call" | custom-call | flops 36864000 | bytes 4096000 | tf_op jit(solution)/shard_map/adjoint/pallas_call | solution.py:386
  29.7 0.0 copy-start.2
  29.7 0.8 %copy-done.2 = f32[128,8,128]{2,1,0:T(8,128)} copy-done((f32[128,8,128]{2,1,0:T(8,128)}, f32[128,8,128]{2,1,0:T(8,128)S(1)}, u32[]{:S(2)}) %copy-start.2) | copy-done | bytes 524312
  30.5 0.0 all-to-all-done.tiles
  30.5 10.7 %all-to-all-start.1 = ((f32[128,8,128]{2,1,0:T(8,128)}), f32[128,8,128]{2,1,0:T(8,128)S(1)}, u32[]{:S(2)}, u32[]{:S(2)}) async-start(f32[128,8,128]{2,1,0:T(8,128)} %copy-done.2), calls=%async_computation.1 | async-start | bytes 1048576 | tf_op jit(solution)/shard_map/all_to_all | solution.py:412
  41.2 9.2 %forward.1 = f32[2,10,40,640]{3,2,1,0:T(8,128)} custom-call(f32[2,10,40,640]{3,2,1,0:T(8,128)} %temp.3, f32[2,40,640]{2,1,0:T(8,128)} %forcing_in.1, f32[43,4,640]{2,1,0:T(4,128)S(1)} %collective-permute-done.a_msg, f32[43,4,640]{2,1,0:T(4,128)S(1)} %collective-permute-done.1.b_msg, s32[40,640]{1,0:T(8,128)S(1)} %copy-done.1, f32[12,10]{1,0:T(8,128)S(1)} %copy-done.3, ...), custom_call_target="tpu_custom_call" | custom-call | flops 36864000 | bytes 4096000 | tf_op jit(solution)/shard_map/forward/pallas_call | solution.py:413
  50.4 4.4 %all-to-all-done.1.received = f32[128,8,128]{2,1,0:T(8,128)S(1)} async-done(((f32[128,8,128]{2,1,0:T(8,128)}), f32[128,8,128]{2,1,0:T(8,128)S(1)}, u32[]{:S(2)}, u32[]{:S(2)}) %all-to-all-start.1) | async-done | bytes 524320 | tf_op jit(solution)/shard_map/all_to_all | solution.py:412
  54.8 0.8 %collect.1 = f32[10,2,32]{2,1,0:T(2,128)} custom-call(f32[128,8,128]{2,1,0:T(8,128)S(1)} %all-to-all-done.1.received), custom_call_target="tpu_custom_call" | custom-call | tf_op jit(solution)/shard_map/collect/pallas_call | solution.py:435
Async XLA Ops:
  0.6 19.8 %copy-start.1 = (s32[40,640]{1,0:T(8,128)S(1)}, s32[40,640]{1,0:T(8,128)}, u32[]{:S(2)}) copy-start(s32[40,640]{1,0:T(8,128)} %soil.5) | copy-start | bytes 307204
  0.6 19.8 %copy-start = (f32[2,10,40,640]{3,2,1,0:T(8,128)S(1)}, f32[2,10,40,640]{3,2,1,0:T(8,128)}, u32[]{:S(2)}) copy-start(f32[2,10,40,640]{3,2,1,0:T(8,128)} %cot.3) | copy-start | bytes 6144004
  0.7 19.8 %copy-start.4 = (s32[16]{0:T(128)S(1)}, s32[16]{0:T(128)}, u32[]{:S(2)}) copy-start(s32[16]{0:T(128)} %tile_map.3) | copy-start | bytes 196
  0.7 19.8 %copy-start.3 = (f32[12,10]{1,0:T(8,128)S(1)}, f32[12,10]{1,0:T(8,128)}, u32[]{:S(2)}) copy-start(f32[12,10]{1,0:T(8,128)} %cond.3) | copy-start | bytes 1444
  3.2 11.4 %collective-permute-start = (f32[43,4,640]{2,1,0:T(4,128)}, f32[43,4,640]{2,1,0:T(4,128)S(1)}, u32[]{:S(2)}, u32[]{:S(2)}) collective-permute-start(f32[43,4,640]{2,1,0:T(4,128)} %get-tuple-element.10), channel_id=1, source_target_pairs={{0,8},{8,0},{16,24},{24,16},{32,40},{40,32},{48,56},{56,48},{64,72... | collective-permute-start | bytes 1320968 | tf_op jit(solution)/shard_map/ppermute | solution.py:381
  4.7 15.8 %collective-permute-start.1 = (f32[43,4,640]{2,1,0:T(4,128)S(1)}, f32[43,4,640]{2,1,0:T(4,128)S(1)}, u32[]{:S(2)}, u32[]{:S(2)}) collective-permute-start(f32[43,4,640]{2,1,0:T(4,128)S(1)} %get-tuple-element.11), channel_id=1, source_target_pairs={{8,16},{24,32},{40,48},{56,64},{72,80},{88,96},{104,112},{16,8},{3... | collective-permute-start | bytes 1320968 | tf_op jit(solution)/shard_map/ppermute | solution.py:382
  9.3 21.1 %all-to-all-start = ((f32[16,8,128]{2,1,0:T(8,128)}), f32[16,8,128]{2,1,0:T(8,128)S(1)}, u32[]{:S(2)}, u32[]{:S(2)}) async-start(f32[16,8,128]{2,1,0:T(8,128)} %get-tuple-element.13), calls=%async_computation | async-start | bytes 131072 | tf_op jit(solution)/shard_map/all_to_all | solution.py:383
  29.7 0.8 %copy-start.2 = (f32[128,8,128]{2,1,0:T(8,128)}, f32[128,8,128]{2,1,0:T(8,128)S(1)}, u32[]{:S(2)}) copy-start(f32[128,8,128]{2,1,0:T(8,128)S(1)} %get-tuple-element.16) | copy-start | bytes 1572868
  30.5 24.3 %all-to-all-start.1 = ((f32[128,8,128]{2,1,0:T(8,128)}), f32[128,8,128]{2,1,0:T(8,128)S(1)}, u32[]{:S(2)}, u32[]{:S(2)}) async-start(f32[128,8,128]{2,1,0:T(8,128)} %copy-done.2), calls=%async_computation.1 | async-start | bytes 1048576 | tf_op jit(solution)/shard_map/all_to_all | solution.py:412

commit v3 on v2

--- a/solution.py
+++ b/solution.py
@@ -387,7 +387,7 @@
         adjoint_kernel,
         out_shape=(
             shape(*cotangent.shape),
-            shape(groups * spaces, 8, LANES),
+            pltpu.HBM((groups * spaces, 8, LANES), f32),
         ),
         in_specs=[VM, VM, VM, VM, SM, SM],
         out_specs=[HB, HB],

time: 55.9 us -> 54.9 us (0.982)
  local copies, waits for them, and re-layouts: 0.81 us -> 0.02 us
    unnamed x10 -> x8, local copies, waits for them, and re-layouts: 0.81 us -> 0.02 us
where the time goes in v3:
time: 54.9 us; the launch traced here: 54.6 us
  starting transfers between devices  22.1 us (40%)
  Pallas kernels  21.6 us (39%)
  waiting for transfers between devices  10.2 us (19%)
  between operations  0.73 us (1%)
    all_to_all x1, starting transfers between devices, body(): received = lax.all_to_all(blocks, ('member', 'space'), 0, 0, tiled=True)  10.7 us
    pallas_call x1, Pallas kernels, body(): pl.pallas_call(forward_kernel, out_shape=shape(*temp_start.shape), in_spe...  9.21 us
    pallas_call x1, Pallas kernels, body(): pl.pallas_call(adjoint_kernel, out_shape=(shape(*cotangent.shape), pltpu....  9.01 us
    ppermute x1, waiting for transfers between devices, body(): b_msg = near(lax.ppermute(b_msg, 'space', across))  5.84 us
    all_to_all x1, starting transfers between devices, body(): tiles = lax.all_to_all(tiles, 'space', 0, 0, tiled=True)  5.27 us
    ppermute x1, starting transfers between devices, body(): b_msg = near(lax.ppermute(b_msg, 'space', across))  4.63 us
    all_to_all x1, waiting for transfers between devices, body(): received = lax.all_to_all(blocks, ('member', 'space'), 0, 0, tiled=True)  4.39 us
    pallas_call x1, Pallas kernels, body(): pl.pallas_call(pack_kernel, out_shape=(shape(total, HALO, cols), shape(to...  2.52 us
  transfers between devices with their start and end apart: 4, of which 2 were waited for; matrix products, arithmetic and copies ran while one was open for 0% of the time, Pallas kernels for 33%

profile of v3, /device:TPU:1, one launch (start us, length us, event | category | flops | bytes accessed | tf_op | source)
XLA Modules:
  0.0 54.6 jit_solution(5541326563450279094)
XLA Ops:
  0.6 0.0 copy-start.1
  0.6 0.0 copy-start
  0.7 0.0 copy-start.3
  0.7 0.0 copy-start.2
  0.7 2.5 %pack.1 = (f32[43,4,640]{2,1,0:T(4,128)}, f32[43,4,640]{2,1,0:T(4,128)S(1)}, f32[16,8,128]{2,1,0:T(8,128)}) custom-call(f32[2,10,40,640]{3,2,1,0:T(8,128)} %cot.3, f32[2,10,40,640]{3,2,1,0:T(8,128)} %temp.3, f32[2,40,640]{2,1,0:T(8,128)} %forcing_in.1, s32[40,640]{1,0:T(8,128)} %soil.5, f32[10,2,32]{2,1,0:T(2,128)} %parent.1), custom_call_target="tpu_custom_call" | custom-call | tf_op jit(solution)/shard_map/pack/pallas_call | solution.py:361
  3.2 1.5 %collective-permute-start = (f32[43,4,640]{2,1,0:T(4,128)}, f32[43,4,640]{2,1,0:T(4,128)S(1)}, u32[]{:S(2)}, u32[]{:S(2)}) collective-permute-start(f32[43,4,640]{2,1,0:T(4,128)} %get-tuple-element.10), channel_id=1, source_target_pairs={{0,8},{8,0},{16,24},{24,16},{32,40},{40,32},{48,56},{56,48},{64,72... | collective-permute-start | bytes 1320968 | tf_op jit(solution)/shard_map/ppermute | solution.py:381
  4.7 4.6 %collective-permute-start.1 = (f32[43,4,640]{2,1,0:T(4,128)S(1)}, f32[43,4,640]{2,1,0:T(4,128)S(1)}, u32[]{:S(2)}, u32[]{:S(2)}) collective-permute-start(f32[43,4,640]{2,1,0:T(4,128)S(1)} %get-tuple-element.11), channel_id=1, source_target_pairs={{8,16},{24,32},{40,48},{56,64},{72,80},{88,96},{104,112},{16,8},{3... | collective-permute-start | bytes 1320968 | tf_op jit(solution)/shard_map/ppermute | solution.py:382
  9.3 5.3 %all-to-all-start = ((f32[16,8,128]{2,1,0:T(8,128)}), f32[16,8,128]{2,1,0:T(8,128)S(1)}, u32[]{:S(2)}, u32[]{:S(2)}) async-start(f32[16,8,128]{2,1,0:T(8,128)} %get-tuple-element.13), calls=%async_computation | async-start | bytes 131072 | tf_op jit(solution)/shard_map/all_to_all | solution.py:383
  14.6 0.0 collective-permute-done.a_msg
  14.6 5.8 %collective-permute-done.1.b_msg = f32[43,4,640]{2,1,0:T(4,128)S(1)} collective-permute-done((f32[43,4,640]{2,1,0:T(4,128)S(1)}, f32[43,4,640]{2,1,0:T(4,128)S(1)}, u32[]{:S(2)}, u32[]{:S(2)}) %collective-permute-start.1) | collective-permute-done | bytes 440352 | tf_op jit(solution)/shard_map/ppermute | solution.py:382
  20.5 0.0 copy-done.1
  20.5 0.0 copy-done
  20.5 0.0 copy-done.3
  20.5 0.0 copy-done.2
  20.5 9.0 %adjoint.1 = (f32[2,10,40,640]{3,2,1,0:T(8,128)}, f32[128,8,128]{2,1,0:T(8,128)}) custom-call(f32[2,10,40,640]{3,2,1,0:T(8,128)S(1)} %copy-done, f32[43,4,640]{2,1,0:T(4,128)S(1)} %collective-permute-done.a_msg, f32[43,4,640]{2,1,0:T(4,128)S(1)} %collective-permute-done.1.b_msg, s32[40,640]{1,0:T(8,128)S(1)} %copy-done.1, f32[12,10]{1,0:T(8,128)S(1)} %copy-done.2, ...), custom_call_target="tpu_custom_call" | custom-call | flops 36864000 | bytes 4096000 | tf_op jit(solution)/shard_map/adjoint/pallas_call | solution.py:386
  29.5 0.0 all-to-all-done.tiles
  29.5 10.7 %all-to-all-start.1 = ((f32[128,8,128]{2,1,0:T(8,128)}), f32[128,8,128]{2,1,0:T(8,128)S(1)}, u32[]{:S(2)}, u32[]{:S(2)}) async-start(f32[128,8,128]{2,1,0:T(8,128)} %get-tuple-element.16), calls=%async_computation.1 | async-start | bytes 1048576 | tf_op jit(solution)/shard_map/all_to_all | solution.py:412
  40.2 9.2 %forward.1 = f32[2,10,40,640]{3,2,1,0:T(8,128)} custom-call(f32[2,10,40,640]{3,2,1,0:T(8,128)} %temp.3, f32[2,40,640]{2,1,0:T(8,128)} %forcing_in.1, f32[43,4,640]{2,1,0:T(4,128)S(1)} %collective-permute-done.a_msg, f32[43,4,640]{2,1,0:T(4,128)S(1)} %collective-permute-done.1.b_msg, s32[40,640]{1,0:T(8,128)S(1)} %copy-done.1, f32[12,10]{1,0:T(8,128)S(1)} %copy-done.2, ...), custom_call_target="tpu_custom_call" | custom-call | flops 36864000 | bytes 4096000 | tf_op jit(solution)/shard_map/forward/pallas_call | solution.py:413
  49.4 4.4 %all-to-all-done.1.received = f32[128,8,128]{2,1,0:T(8,128)S(1)} async-done(((f32[128,8,128]{2,1,0:T(8,128)}), f32[128,8,128]{2,1,0:T(8,128)S(1)}, u32[]{:S(2)}, u32[]{:S(2)}) %all-to-all-start.1) | async-done | bytes 524320 | tf_op jit(solution)/shard_map/all_to_all | solution.py:412
  53.8 0.8 %collect.1 = f32[10,2,32]{2,1,0:T(2,128)} custom-call(f32[128,8,128]{2,1,0:T(8,128)S(1)} %all-to-all-done.1.received), custom_call_target="tpu_custom_call" | custom-call | tf_op jit(solution)/shard_map/collect/pallas_call | solution.py:435
Async XLA Ops:
  0.6 19.8 %copy-start.1 = (s32[40,640]{1,0:T(8,128)S(1)}, s32[40,640]{1,0:T(8,128)}, u32[]{:S(2)}) copy-start(s32[40,640]{1,0:T(8,128)} %soil.5) | copy-start | bytes 307204
  0.6 19.8 %copy-start = (f32[2,10,40,640]{3,2,1,0:T(8,128)S(1)}, f32[2,10,40,640]{3,2,1,0:T(8,128)}, u32[]{:S(2)}) copy-start(f32[2,10,40,640]{3,2,1,0:T(8,128)} %cot.3) | copy-start | bytes 6144004
  0.7 19.8 %copy-start.3 = (s32[16]{0:T(128)S(1)}, s32[16]{0:T(128)}, u32[]{:S(2)}) copy-start(s32[16]{0:T(128)} %tile_map.3) | copy-start | bytes 196
  0.7 19.8 %copy-start.2 = (f32[12,10]{1,0:T(8,128)S(1)}, f32[12,10]{1,0:T(8,128)}, u32[]{:S(2)}) copy-start(f32[12,10]{1,0:T(8,128)} %cond.3) | copy-start | bytes 1444
  3.2 11.4 %collective-permute-start = (f32[43,4,640]{2,1,0:T(4,128)}, f32[43,4,640]{2,1,0:T(4,128)S(1)}, u32[]{:S(2)}, u32[]{:S(2)}) collective-permute-start(f32[43,4,640]{2,1,0:T(4,128)} %get-tuple-element.10), channel_id=1, source_target_pairs={{0,8},{8,0},{16,24},{24,16},{32,40},{40,32},{48,56},{56,48},{64,72... | collective-permute-start | bytes 1320968 | tf_op jit(solution)/shard_map/ppermute | solution.py:381
  4.7 15.8 %collective-permute-start.1 = (f32[43,4,640]{2,1,0:T(4,128)S(1)}, f32[43,4,640]{2,1,0:T(4,128)S(1)}, u32[]{:S(2)}, u32[]{:S(2)}) collective-permute-start(f32[43,4,640]{2,1,0:T(4,128)S(1)} %get-tuple-element.11), channel_id=1, source_target_pairs={{8,16},{24,32},{40,48},{56,64},{72,80},{88,96},{104,112},{16,8},{3... | collective-permute-start | bytes 1320968 | tf_op jit(solution)/shard_map/ppermute | solution.py:382
  9.3 20.2 %all-to-all-start = ((f32[16,8,128]{2,1,0:T(8,128)}), f32[16,8,128]{2,1,0:T(8,128)S(1)}, u32[]{:S(2)}, u32[]{:S(2)}) async-start(f32[16,8,128]{2,1,0:T(8,128)} %get-tuple-element.13), calls=%async_computation | async-start | bytes 131072 | tf_op jit(solution)/shard_map/all_to_all | solution.py:383
  29.5 24.3 %all-to-all-start.1 = ((f32[128,8,128]{2,1,0:T(8,128)}), f32[128,8,128]{2,1,0:T(8,128)S(1)}, u32[]{:S(2)}, u32[]{:S(2)}) async-start(f32[128,8,128]{2,1,0:T(8,128)} %get-tuple-element.16), calls=%async_computation.1 | async-start | bytes 1048576 | tf_op jit(solution)/shard_map/all_to_all | solution.py:412
